TPU v7x, 512 devices: a whole 4x8x8 slice. The times are simulated.
512 devices in a mesh: parts: 512 (over x, z, y, core).
Axes of the slice: x: 4, y: 8, z: 8, core: 2. Of those that a mesh axis runs over, the one named last changes fastest.
Arguments:
- rhs_partial: float32 [3, 739840], P(None, 'parts'), may hold values from -12 to 12
- connectivity: int32 [27, 65536], P(None, 'parts'), may hold values from 0 to 1444, as said below
- hessians: bfloat16 [45, 27, 65536], P(None, None, 'parts'), may hold values from -1 to 3, as said below
- shared_nodes: int32 [8, 17408], P(None, 'parts'), may hold values from 0 to 1445, as said below
- owner: int32 [739840], P('parts'), may hold values from 0 to 1, as said below
Outputs:
- solution: float32 [3, 739840], P(None, 'parts')
- residual: float32 [3, 739840], P(None, 'parts')
Inputs may be any that keep to these rules, and one draw needn't show every extreme that they name: `connectivity`: local node numbers of the element's own partition; each partition's elements form a conforming block of 8 x 8 x 2 elements that share their common nodes. `hessians`: each 9 x 9 matrix is positive definite. `shared_nodes`: the rows of two neighbouring partitions for each other name the same physical nodes in the same order and are equally long; a local node is in at most one row, and only nodes on the block's boundary are in rows; used slots come first and unused slots hold 1445; in every draw some row of some partition has all 34 slots used. `owner`: 1 on every node in no row of shared_nodes, and on exactly one of the two copies of each shared node.
All inputs are finite; a program needn't handle non-finite values.
Results may differ from a plain program's by a relative error of at most 0.0003.
Values sent between devices are 32-bit elements; how exact they have to be, the bound alone decides.
A program may use at most 64 MiB of HBM per device.

v0:
```python
import jax
import jax.numpy as jnp
import numpy as np
from jax import lax
from jax.sharding import PartitionSpec as P

ITERS = 5


DAMPING = 2.0


def shifted(block, axis, distance):
    devices = range(lax.axis_size(axis))
    route = [((i - distance) % len(devices), i) for i in devices]
    return lax.ppermute(block, axis, route)


def shape_table():
    points = np.array([-np.sqrt(0.6), 0.0, np.sqrt(0.6)])
    values = np.stack(
        [points * (points - 1.0) / 2.0, 1.0 - points * points, points * (points + 1.0) / 2.0],
        axis=1,
    )
    slopes = np.stack([points - 0.5, -2.0 * points, points + 0.5], axis=1)
    result = np.zeros((27, 3, 27))
    for direction in range(3):
        factors = [slopes if axis_index == direction else values for axis_index in range(3)]
        product = (
            factors[0][:, None, None, :, None, None]
            * factors[1][None, :, None, None, :, None]
            * factors[2][None, None, :, None, None, :]
        )
        result[:, direction, :] = product.reshape(27, 27)
    return jnp.asarray(result.reshape(81, 27), dtype=jnp.float32)


def packed_index(row_index, col_index):
    first = min(row_index, col_index)
    second = max(row_index, col_index)
    return first * 9 - first * (first - 1) // 2 + (second - first)


def apply_local(field, element_nodes, element_hessians):
    table = shape_table()
    elements = element_nodes.shape[1]
    node_count = field.shape[1]
    element_values = jnp.take(field, element_nodes, axis=1)
    element_values = jnp.transpose(element_values, (1, 0, 2)).reshape(27, 3 * elements)
    gradients = jnp.dot(table, element_values, precision=lax.Precision.HIGHEST).reshape(
        27, 3, 3, elements
    )
    components = [gradients[:, col_index % 3, col_index // 3, :] for col_index in range(9)]
    entries = [element_hessians[entry].astype(jnp.float32) for entry in range(45)]
    stresses = []
    for row_index in range(9):
        accumulated = entries[packed_index(row_index, 0)] * components[0]
        for col_index in range(1, 9):
            accumulated = (
                accumulated + entries[packed_index(row_index, col_index)] * components[col_index]
            )
        stresses.append(accumulated)
    stress = jnp.stack(stresses, 0).reshape(3, 3, 27, elements)
    stress = jnp.transpose(stress, (2, 1, 0, 3)).reshape(81, 3 * elements)
    element_terms = jnp.dot(table.T, stress, precision=lax.Precision.HIGHEST).reshape(
        27, 3, elements
    )
    summed = jnp.zeros((3, node_count), jnp.float32)
    return summed.at[:, element_nodes].add(jnp.transpose(element_terms, (1, 0, 2)))


def peer_offsets(count):
    half = count // 2
    return [offset - half for offset in range(half)] + [offset + 1 for offset in range(half)]


def assemble(partial_value, shared_lists):
    count = shared_lists.shape[0]
    offsets = peer_offsets(count)
    outgoing = jnp.take(partial_value, shared_lists, axis=1, mode="fill", fill_value=0.0)
    outgoing = jnp.transpose(outgoing, (1, 0, 2))
    incoming_rows = [None] * count
    for row_index in range(count):
        arrived = shifted(outgoing[row_index], "parts", offsets[row_index])
        incoming_rows[count - 1 - row_index] = arrived
    incoming = jnp.stack(incoming_rows, 0)
    return partial_value.at[:, shared_lists].add(jnp.transpose(incoming, (1, 0, 2)), mode="drop")


def shards(rhs_partial, connectivity, hessians, shared_nodes, owner):
    owned_mask = owner.astype(jnp.float32)[None, :]

    def local_inner(first_field, second_field):
        return jnp.sum(owned_mask * first_field * second_field)

    def squares_sum(field):
        return lax.psum(local_inner(field, field), "parts")

    rhs = assemble(rhs_partial, shared_nodes)
    solution = jnp.zeros_like(rhs)
    residual = rhs
    direction = rhs
    norm_now = squares_sum(residual)
    for iteration in range(ITERS):
        image = (
            assemble(apply_local(direction, connectivity, hessians), shared_nodes)
            + DAMPING * direction
        )
        step_size = norm_now / lax.psum(local_inner(direction, image), "parts")
        solution = solution + step_size * direction
        residual = residual - step_size * image
        norm_next = squares_sum(residual)
        direction = residual + norm_next / norm_now * direction
        norm_now = norm_next
    return (solution, residual)


def solution(mesh):
    in_specs = (
        P(None, "parts"),
        P(None, "parts"),
        P(None, None, "parts"),
        P(None, "parts"),
        P("parts"),
    )
    out_specs = (P(None, "parts"), P(None, "parts"))
    return jax.shard_map(shards, mesh=mesh, in_specs=in_specs, out_specs=out_specs, check_vma=False)
```

profile of v0, /device:TPU:1, one launch (start us, length us, event | category | flops | bytes accessed | tf_op | source)
XLA Modules:
  0.0 1262.9 jit_solution(11818860398895166302)
XLA Ops:
  4.4 5.0 collective-permute-start
  9.5 6.3 collective-permute-start.1
  24.6 8.9 collective-permute-start.5
  33.6 5.5 collective-permute-start.6
  39.1 5.8 collective-permute-start.7
  48.5 5.8 gather_fusion.1
  58.3 20.1 %scatter_custom_fusion.1 = f32[3,1445]{0,1:T(8,128)S(1)} fusion(s32[3456]{0:T(1024)S(1)} %fusion.16, f32[3456,3]{1,0:T(8,128)S(1)} %copy.257, f32[]{:T(128)} %constant.23.clone.1), kind=kCustom, calls=%fused_computation.30 | custom fusion | flops 10368 | bytes 17344 | tf_op jit(solution)/shard_map/scatter-add | solution.py:69
  86.0 2.5 collective-permute-start.11
  91.0 8.7 collective-permute-start.13
  99.6 5.2 collective-permute-start.14
  104.8 5.8 collective-permute-start.15
  114.8 98.0 %all-reduce = (f32[]{:T(128)}, f32[]{:T(128)}) all-reduce(f32[]{:T(128)} %get-tuple-element.11, f32[]{:T(128)} %get-tuple-element.10), channel_id=1, replica_groups=mesh['parts'=512] {'parts'}, use_global_device_ids=true, to_apply=%region_2.4 | all-reduce | flops 2 | bytes 16 | tf_op jit(solution)/shard_map/psum | solution.py:97
  214.7 94.3 %psum.72 = f32[]{:T(128)} all-reduce(f32[]{:T(128)} %fusion.12), channel_id=1, replica_groups=mesh['parts'=512] {'parts'}, use_global_device_ids=true, to_apply=%region_8.11 | all-reduce | flops 1 | bytes 8 | tf_op jit(solution)/shard_map/psum | solution.py:97
  310.7 5.8 gather_fusion.3
  320.5 20.1 %scatter_custom_fusion.3 = f32[3,1445]{0,1:T(8,128)S(1)} fusion(s32[3456]{0:T(1024)S(1)} %fusion.16, f32[3456,3]{1,0:T(8,128)S(1)} %copy.282, f32[]{:T(128)} %constant.23.clone.1), kind=kCustom, calls=%fused_computation.28 | custom fusion | flops 10368 | bytes 17344 | tf_op jit(solution)/shard_map/scatter-add | solution.py:69
  342.3 2.8 collective-permute-start.16
  345.1 5.6 collective-permute-start.17
  357.5 8.6 collective-permute-start.21
  366.1 2.4 collective-permute-start.22
  368.5 4.0 collective-permute-start.23
  377.2 97.4 %psum.73 = f32[]{:T(128)} all-reduce(f32[]{:T(128)} %multiply_reduce_fusion.3), channel_id=1, replica_groups=mesh['parts'=512] {'parts'}, use_global_device_ids=true, to_apply=%region_12.15 | all-reduce | flops 1 | bytes 8 | tf_op jit(solution)/shard_map/psum | solution.py:109
  476.6 94.5 %psum.74 = f32[]{:T(128)} all-reduce(f32[]{:T(128)} %get-tuple-element.18), channel_id=1, replica_groups=mesh['parts'=512] {'parts'}, use_global_device_ids=true, to_apply=%region_14.17 | all-reduce | flops 1 | bytes 8 | tf_op jit(solution)/shard_map/psum | solution.py:97
  572.8 5.8 gather_fusion.5
  582.5 20.1 %scatter_custom_fusion.5 = f32[3,1445]{0,1:T(8,128)S(1)} fusion(s32[3456]{0:T(1024)S(1)} %fusion.16, f32[3456,3]{1,0:T(8,128)S(1)} %copy.303, f32[]{:T(128)} %constant.23.clone.1), kind=kCustom, calls=%fused_computation.26 | custom fusion | flops 10368 | bytes 17344 | tf_op jit(solution)/shard_map/scatter-add | solution.py:69
  604.3 2.6 collective-permute-start.24
  607.0 5.6 collective-permute-start.25
  619.4 8.5 collective-permute-start.29
  628.0 2.4 collective-permute-start.30
  630.4 4.1 collective-permute-start.31
  639.1 97.4 %psum.75 = f32[]{:T(128)} all-reduce(f32[]{:T(128)} %multiply_reduce_fusion.2), channel_id=1, replica_groups=mesh['parts'=512] {'parts'}, use_global_device_ids=true, to_apply=%region_18.21 | all-reduce | flops 1 | bytes 8 | tf_op jit(solution)/shard_map/psum | solution.py:109
  738.6 94.7 %psum.76 = f32[]{:T(128)} all-reduce(f32[]{:T(128)} %get-tuple-element.16), channel_id=1, replica_groups=mesh['parts'=512] {'parts'}, use_global_device_ids=true, to_apply=%region_20.23 | all-reduce | flops 1 | bytes 8 | tf_op jit(solution)/shard_map/psum | solution.py:97
  834.9 5.8 gather_fusion.7
  844.7 20.1 %scatter_custom_fusion.7 = f32[3,1445]{0,1:T(8,128)S(1)} fusion(s32[3456]{0:T(1024)S(1)} %fusion.16, f32[3456,3]{1,0:T(8,128)S(1)} %copy.324, f32[]{:T(128)} %constant.23.clone.1), kind=kCustom, calls=%fused_computation.24 | custom fusion | flops 10368 | bytes 17344 | tf_op jit(solution)/shard_map/scatter-add | solution.py:69
  866.5 2.7 collective-permute-start.32
  869.2 5.6 collective-permute-start.33
  881.6 8.6 collective-permute-start.37
  890.2 2.4 collective-permute-start.38
  892.6 4.1 collective-permute-start.39
  901.4 97.4 %psum.77 = f32[]{:T(128)} all-reduce(f32[]{:T(128)} %multiply_reduce_fusion.1), channel_id=1, replica_groups=mesh['parts'=512] {'parts'}, use_global_device_ids=true, to_apply=%region_24.27 | all-reduce | flops 1 | bytes 8 | tf_op jit(solution)/shard_map/psum | solution.py:109
  1000.7 94.5 %psum.78 = f32[]{:T(128)} all-reduce(f32[]{:T(128)} %get-tuple-element.14), channel_id=1, replica_groups=mesh['parts'=512] {'parts'}, use_global_device_ids=true, to_apply=%region_26.29 | all-reduce | flops 1 | bytes 8 | tf_op jit(solution)/shard_map/psum | solution.py:97
  1096.9 5.8 gather_fusion.9
  1106.6 20.1 %scatter_custom_fusion.9 = f32[3,1445]{0,1:T(8,128)S(1)} fusion(s32[3456]{0:T(1024)S(1)} %fusion.16, f32[3456,3]{1,0:T(8,128)S(1)} %copy.345, f32[]{:T(128)} %constant.23.clone.1), kind=kCustom, calls=%fused_computation.22 | custom fusion | flops 10368 | bytes 17344 | tf_op jit(solution)/shard_map/scatter-add | solution.py:69
  1128.4 2.6 collective-permute-start.40
  1131.0 5.6 collective-permute-start.41
  1143.5 8.5 collective-permute-start.45
  1152.0 2.5 collective-permute-start.46
  1154.6 4.0 collective-permute-start.47
  1163.3 97.4 %psum.79 = f32[]{:T(128)} all-reduce(f32[]{:T(128)} %multiply_reduce_fusion), channel_id=1, replica_groups=mesh['parts'=512] {'parts'}, use_global_device_ids=true, to_apply=%region_30.33 | all-reduce | flops 1 | bytes 8 | tf_op jit(solution)/shard_map/psum | solution.py:109
  (384 shorter events, 105.4 us)
Async XLA Ops:
  4.4 20.2 %collective-permute-start = (f32[3,34]{1,0:T(4,128)S(1)}, f32[3,34]{1,0:T(4,128)S(1)}, u32[]{:S(2)}, u32[]{:S(2)}) collective-permute-start(f32[3,34]{1,0:T(4,128)S(1)} %bitcast.1482), channel_id=1, source_target_pairs={{508,0},{509,1},{510,2},{511,3},{0,4},{1,5},{2,6},{3,7},{4,8},{5,9... | collective-permute-start | bytes 1232 | tf_op jit(solution)/shard_map/ppermute | solution.py:16
  9.5 24.1 %collective-permute-start.1 = (f32[3,34]{1,0:T(4,128)S(1)}, f32[3,34]{1,0:T(4,128)S(1)}, u32[]{:S(2)}, u32[]{:S(2)}) collective-permute-start(f32[3,34]{1,0:T(4,128)S(1)} %bitcast.1481), channel_id=1, source_target_pairs={{509,0},{510,1},{511,2},{0,3},{1,4},{2,5},{3,6},{4,7},{5,8},{6,9},... | collective-permute-start | bytes 1232 | tf_op jit(solution)/shard_map/ppermute | solution.py:16
  15.8 23.4 %collective-permute-start.2 = (f32[3,34]{1,0:T(4,128)S(1)}, f32[3,34]{1,0:T(4,128)S(1)}, u32[]{:S(2)}, u32[]{:S(2)}) collective-permute-start(f32[3,34]{1,0:T(4,128)S(1)} %bitcast.1475), channel_id=1, source_target_pairs={{510,0},{511,1},{0,2},{1,3},{2,4},{3,5},{4,6},{5,7},{6,8},{7,9},{8... | collective-permute-start | bytes 1232 | tf_op jit(solution)/shard_map/ppermute | solution.py:16
  18.1 26.8 %collective-permute-start.3 = (f32[3,34]{1,0:T(4,128)S(1)}, f32[3,34]{1,0:T(4,128)S(1)}, u32[]{:S(2)}, u32[]{:S(2)}) collective-permute-start(f32[3,34]{1,0:T(4,128)S(1)} %bitcast.1473), channel_id=1, source_target_pairs={{511,0},{0,1},{1,2},{2,3},{3,4},{4,5},{5,6},{6,7},{7,8},{8,9},{9,1... | collective-permute-start | bytes 1232 | tf_op jit(solution)/shard_map/ppermute | solution.py:16
  20.2 24.7 %collective-permute-start.4 = (f32[3,34]{1,0:T(4,128)S(1)}, f32[3,34]{1,0:T(4,128)S(1)}, u32[]{:S(2)}, u32[]{:S(2)}) collective-permute-start(f32[3,34]{1,0:T(4,128)S(1)} %bitcast.1472), channel_id=1, source_target_pairs={{1,0},{2,1},{3,2},{4,3},{5,4},{6,5},{7,6},{8,7},{9,8},{10,9},{11,1... | collective-permute-start | bytes 1232 | tf_op jit(solution)/shard_map/ppermute | solution.py:16
  24.6 20.3 %collective-permute-start.5 = (f32[3,34]{1,0:T(4,128)S(1)}, f32[3,34]{1,0:T(4,128)S(1)}, u32[]{:S(2)}, u32[]{:S(2)}) collective-permute-start(f32[3,34]{1,0:T(4,128)S(1)} %bitcast.1480), channel_id=1, source_target_pairs={{2,0},{3,1},{4,2},{5,3},{6,4},{7,5},{8,6},{9,7},{10,8},{11,9},{12,... | collective-permute-start | bytes 1232 | tf_op jit(solution)/shard_map/ppermute | solution.py:16
  33.6 11.4 collective-permute-start.6
  39.1 6.5 collective-permute-start.7
  80.1 10.9 collective-permute-start.8
  82.0 17.6 %collective-permute-start.9 = (f32[3,34]{1,0:T(4,128)S(1)}, f32[3,34]{1,0:T(4,128)S(1)}, u32[]{:S(2)}, u32[]{:S(2)}) collective-permute-start(f32[3,34]{1,0:T(4,128)S(1)} %bitcast.1483), channel_id=1, source_target_pairs={{509,0},{510,1},{511,2},{0,3},{1,4},{2,5},{3,6},{4,7},{5,8},{6,9},... | collective-permute-start | bytes 1232 | tf_op jit(solution)/shard_map/ppermute | solution.py:16
  84.0 20.8 %collective-permute-start.10 = (f32[3,34]{1,0:T(4,128)S(1)}, f32[3,34]{1,0:T(4,128)S(1)}, u32[]{:S(2)}, u32[]{:S(2)}) collective-permute-start(f32[3,34]{1,0:T(4,128)S(1)} %bitcast.1474), channel_id=1, source_target_pairs={{510,0},{511,1},{0,2},{1,3},{2,4},{3,5},{4,6},{5,7},{6,8},{7,9},{8... | collective-permute-start | bytes 1232 | tf_op jit(solution)/shard_map/ppermute | solution.py:16
  86.0 24.6 %collective-permute-start.11 = (f32[3,34]{1,0:T(4,128)S(1)}, f32[3,34]{1,0:T(4,128)S(1)}, u32[]{:S(2)}, u32[]{:S(2)}) collective-permute-start(f32[3,34]{1,0:T(4,128)S(1)} %bitcast.1466), channel_id=1, source_target_pairs={{511,0},{0,1},{1,2},{2,3},{3,4},{4,5},{5,6},{6,7},{7,8},{8,9},{9,1... | collective-permute-start | bytes 1232 | tf_op jit(solution)/shard_map/ppermute | solution.py:16
  88.5 22.2 %collective-permute-start.12 = (f32[3,34]{1,0:T(4,128)S(1)}, f32[3,34]{1,0:T(4,128)S(1)}, u32[]{:S(2)}, u32[]{:S(2)}) collective-permute-start(f32[3,34]{1,0:T(4,128)S(1)} %bitcast.1460), channel_id=1, source_target_pairs={{1,0},{2,1},{3,2},{4,3},{5,4},{6,5},{7,6},{8,7},{9,8},{10,9},{11,1... | collective-permute-start | bytes 1232 | tf_op jit(solution)/shard_map/ppermute | solution.py:16
  91.0 19.7 %collective-permute-start.13 = (f32[3,34]{1,0:T(4,128)S(1)}, f32[3,34]{1,0:T(4,128)S(1)}, u32[]{:S(2)}, u32[]{:S(2)}) collective-permute-start(f32[3,34]{1,0:T(4,128)S(1)} %bitcast.1455), channel_id=1, source_target_pairs={{2,0},{3,1},{4,2},{5,3},{6,4},{7,5},{8,6},{9,7},{10,8},{11,9},{12,... | collective-permute-start | bytes 1232 | tf_op jit(solution)/shard_map/ppermute | solution.py:16
  99.6 11.1 collective-permute-start.14
  104.8 6.5 collective-permute-start.15
  342.3 15.2 %collective-permute-start.16 = (f32[3,34]{1,0:T(4,128)S(1)}, f32[3,34]{1,0:T(4,128)S(1)}, u32[]{:S(2)}, u32[]{:S(2)}) collective-permute-start(f32[3,34]{1,0:T(4,128)S(1)} %bitcast.1489), channel_id=1, source_target_pairs={{508,0},{509,1},{510,2},{511,3},{0,4},{1,5},{2,6},{3,7},{4,8},{5,9... | collective-permute-start | bytes 1232 | tf_op jit(solution)/shard_map/ppermute | solution.py:16
  345.1 21.0 %collective-permute-start.17 = (f32[3,34]{1,0:T(4,128)S(1)}, f32[3,34]{1,0:T(4,128)S(1)}, u32[]{:S(2)}, u32[]{:S(2)}) collective-permute-start(f32[3,34]{1,0:T(4,128)S(1)} %bitcast.1484), channel_id=1, source_target_pairs={{509,0},{510,1},{511,2},{0,3},{1,4},{2,5},{3,6},{4,7},{5,8},{6,9},... | collective-permute-start | bytes 1232 | tf_op jit(solution)/shard_map/ppermute | solution.py:16
  350.7 17.8 %collective-permute-start.18 = (f32[3,34]{1,0:T(4,128)S(1)}, f32[3,34]{1,0:T(4,128)S(1)}, u32[]{:S(2)}, u32[]{:S(2)}) collective-permute-start(f32[3,34]{1,0:T(4,128)S(1)} %bitcast.1476), channel_id=1, source_target_pairs={{510,0},{511,1},{0,2},{1,3},{2,4},{3,5},{4,6},{5,7},{6,8},{7,9},{8... | collective-permute-start | bytes 1232 | tf_op jit(solution)/shard_map/ppermute | solution.py:16
  352.8 19.7 %collective-permute-start.19 = (f32[3,34]{1,0:T(4,128)S(1)}, f32[3,34]{1,0:T(4,128)S(1)}, u32[]{:S(2)}, u32[]{:S(2)}) collective-permute-start(f32[3,34]{1,0:T(4,128)S(1)} %bitcast.1467), channel_id=1, source_target_pairs={{511,0},{0,1},{1,2},{2,3},{3,4},{4,5},{5,6},{6,7},{7,8},{8,9},{9,1... | collective-permute-start | bytes 1232 | tf_op jit(solution)/shard_map/ppermute | solution.py:16
  355.1 17.4 %collective-permute-start.20 = (f32[3,34]{1,0:T(4,128)S(1)}, f32[3,34]{1,0:T(4,128)S(1)}, u32[]{:S(2)}, u32[]{:S(2)}) collective-permute-start(f32[3,34]{1,0:T(4,128)S(1)} %bitcast.1461), channel_id=1, source_target_pairs={{1,0},{2,1},{3,2},{4,3},{5,4},{6,5},{7,6},{8,7},{9,8},{10,9},{11,1... | collective-permute-start | bytes 1232 | tf_op jit(solution)/shard_map/ppermute | solution.py:16
  357.5 15.1 %collective-permute-start.21 = (f32[3,34]{1,0:T(4,128)S(1)}, f32[3,34]{1,0:T(4,128)S(1)}, u32[]{:S(2)}, u32[]{:S(2)}) collective-permute-start(f32[3,34]{1,0:T(4,128)S(1)} %bitcast.1456), channel_id=1, source_target_pairs={{2,0},{3,1},{4,2},{5,3},{6,4},{7,5},{8,6},{9,7},{10,8},{11,9},{12,... | collective-permute-start | bytes 1232 | tf_op jit(solution)/shard_map/ppermute | solution.py:16
  366.1 6.5 collective-permute-start.22
  368.5 5.2 collective-permute-start.23
  604.3 15.1 %collective-permute-start.24 = (f32[3,34]{1,0:T(4,128)S(1)}, f32[3,34]{1,0:T(4,128)S(1)}, u32[]{:S(2)}, u32[]{:S(2)}) collective-permute-start(f32[3,34]{1,0:T(4,128)S(1)} %bitcast.1490), channel_id=1, source_target_pairs={{508,0},{509,1},{510,2},{511,3},{0,4},{1,5},{2,6},{3,7},{4,8},{5,9... | collective-permute-start | bytes 1232 | tf_op jit(solution)/shard_map/ppermute | solution.py:16
  607.0 21.0 %collective-permute-start.25 = (f32[3,34]{1,0:T(4,128)S(1)}, f32[3,34]{1,0:T(4,128)S(1)}, u32[]{:S(2)}, u32[]{:S(2)}) collective-permute-start(f32[3,34]{1,0:T(4,128)S(1)} %bitcast.1485), channel_id=1, source_target_pairs={{509,0},{510,1},{511,2},{0,3},{1,4},{2,5},{3,6},{4,7},{5,8},{6,9},... | collective-permute-start | bytes 1232 | tf_op jit(solution)/shard_map/ppermute | solution.py:16
  612.6 17.8 %collective-permute-start.26 = (f32[3,34]{1,0:T(4,128)S(1)}, f32[3,34]{1,0:T(4,128)S(1)}, u32[]{:S(2)}, u32[]{:S(2)}) collective-permute-start(f32[3,34]{1,0:T(4,128)S(1)} %bitcast.1477), channel_id=1, source_target_pairs={{510,0},{511,1},{0,2},{1,3},{2,4},{3,5},{4,6},{5,7},{6,8},{7,9},{8... | collective-permute-start | bytes 1232 | tf_op jit(solution)/shard_map/ppermute | solution.py:16
  614.8 19.8 %collective-permute-start.27 = (f32[3,34]{1,0:T(4,128)S(1)}, f32[3,34]{1,0:T(4,128)S(1)}, u32[]{:S(2)}, u32[]{:S(2)}) collective-permute-start(f32[3,34]{1,0:T(4,128)S(1)} %bitcast.1468), channel_id=1, source_target_pairs={{511,0},{0,1},{1,2},{2,3},{3,4},{4,5},{5,6},{6,7},{7,8},{8,9},{9,1... | collective-permute-start | bytes 1232 | tf_op jit(solution)/shard_map/ppermute | solution.py:16
  617.0 17.6 %collective-permute-start.28 = (f32[3,34]{1,0:T(4,128)S(1)}, f32[3,34]{1,0:T(4,128)S(1)}, u32[]{:S(2)}, u32[]{:S(2)}) collective-permute-start(f32[3,34]{1,0:T(4,128)S(1)} %bitcast.1462), channel_id=1, source_target_pairs={{1,0},{2,1},{3,2},{4,3},{5,4},{6,5},{7,6},{8,7},{9,8},{10,9},{11,1... | collective-permute-start | bytes 1232 | tf_op jit(solution)/shard_map/ppermute | solution.py:16
  619.4 15.2 %collective-permute-start.29 = (f32[3,34]{1,0:T(4,128)S(1)}, f32[3,34]{1,0:T(4,128)S(1)}, u32[]{:S(2)}, u32[]{:S(2)}) collective-permute-start(f32[3,34]{1,0:T(4,128)S(1)} %bitcast.1457), channel_id=1, source_target_pairs={{2,0},{3,1},{4,2},{5,3},{6,4},{7,5},{8,6},{9,7},{10,8},{11,9},{12,... | collective-permute-start | bytes 1232 | tf_op jit(solution)/shard_map/ppermute | solution.py:16
  628.0 6.6 collective-permute-start.30
  630.4 5.2 collective-permute-start.31
  866.5 15.1 %collective-permute-start.32 = (f32[3,34]{1,0:T(4,128)S(1)}, f32[3,34]{1,0:T(4,128)S(1)}, u32[]{:S(2)}, u32[]{:S(2)}) collective-permute-start(f32[3,34]{1,0:T(4,128)S(1)} %bitcast.1491), channel_id=1, source_target_pairs={{508,0},{509,1},{510,2},{511,3},{0,4},{1,5},{2,6},{3,7},{4,8},{5,9... | collective-permute-start | bytes 1232 | tf_op jit(solution)/shard_map/ppermute | solution.py:16
  869.2 21.0 %collective-permute-start.33 = (f32[3,34]{1,0:T(4,128)S(1)}, f32[3,34]{1,0:T(4,128)S(1)}, u32[]{:S(2)}, u32[]{:S(2)}) collective-permute-start(f32[3,34]{1,0:T(4,128)S(1)} %bitcast.1486), channel_id=1, source_target_pairs={{509,0},{510,1},{511,2},{0,3},{1,4},{2,5},{3,6},{4,7},{5,8},{6,9},... | collective-permute-start | bytes 1232 | tf_op jit(solution)/shard_map/ppermute | solution.py:16
  874.8 17.8 %collective-permute-start.34 = (f32[3,34]{1,0:T(4,128)S(1)}, f32[3,34]{1,0:T(4,128)S(1)}, u32[]{:S(2)}, u32[]{:S(2)}) collective-permute-start(f32[3,34]{1,0:T(4,128)S(1)} %bitcast.1478), channel_id=1, source_target_pairs={{510,0},{511,1},{0,2},{1,3},{2,4},{3,5},{4,6},{5,7},{6,8},{7,9},{8... | collective-permute-start | bytes 1232 | tf_op jit(solution)/shard_map/ppermute | solution.py:16
  877.0 19.7 %collective-permute-start.35 = (f32[3,34]{1,0:T(4,128)S(1)}, f32[3,34]{1,0:T(4,128)S(1)}, u32[]{:S(2)}, u32[]{:S(2)}) collective-permute-start(f32[3,34]{1,0:T(4,128)S(1)} %bitcast.1469), channel_id=1, source_target_pairs={{511,0},{0,1},{1,2},{2,3},{3,4},{4,5},{5,6},{6,7},{7,8},{8,9},{9,1... | collective-permute-start | bytes 1232 | tf_op jit(solution)/shard_map/ppermute | solution.py:16
  879.2 17.5 %collective-permute-start.36 = (f32[3,34]{1,0:T(4,128)S(1)}, f32[3,34]{1,0:T(4,128)S(1)}, u32[]{:S(2)}, u32[]{:S(2)}) collective-permute-start(f32[3,34]{1,0:T(4,128)S(1)} %bitcast.1463), channel_id=1, source_target_pairs={{1,0},{2,1},{3,2},{4,3},{5,4},{6,5},{7,6},{8,7},{9,8},{10,9},{11,1... | collective-permute-start | bytes 1232 | tf_op jit(solution)/shard_map/ppermute | solution.py:16
  881.6 15.1 %collective-permute-start.37 = (f32[3,34]{1,0:T(4,128)S(1)}, f32[3,34]{1,0:T(4,128)S(1)}, u32[]{:S(2)}, u32[]{:S(2)}) collective-permute-start(f32[3,34]{1,0:T(4,128)S(1)} %bitcast.1458), channel_id=1, source_target_pairs={{2,0},{3,1},{4,2},{5,3},{6,4},{7,5},{8,6},{9,7},{10,8},{11,9},{12,... | collective-permute-start | bytes 1232 | tf_op jit(solution)/shard_map/ppermute | solution.py:16
  890.2 6.6 collective-permute-start.38
  892.6 5.2 collective-permute-start.39
  1128.4 15.1 %collective-permute-start.40 = (f32[3,34]{1,0:T(4,128)S(1)}, f32[3,34]{1,0:T(4,128)S(1)}, u32[]{:S(2)}, u32[]{:S(2)}) collective-permute-start(f32[3,34]{1,0:T(4,128)S(1)} %bitcast.1492), channel_id=1, source_target_pairs={{508,0},{509,1},{510,2},{511,3},{0,4},{1,5},{2,6},{3,7},{4,8},{5,9... | collective-permute-start | bytes 1232 | tf_op jit(solution)/shard_map/ppermute | solution.py:16
  1131.0 21.0 %collective-permute-start.41 = (f32[3,34]{1,0:T(4,128)S(1)}, f32[3,34]{1,0:T(4,128)S(1)}, u32[]{:S(2)}, u32[]{:S(2)}) collective-permute-start(f32[3,34]{1,0:T(4,128)S(1)} %bitcast.1487), channel_id=1, source_target_pairs={{509,0},{510,1},{511,2},{0,3},{1,4},{2,5},{3,6},{4,7},{5,8},{6,9},... | collective-permute-start | bytes 1232 | tf_op jit(solution)/shard_map/ppermute | solution.py:16
  1136.6 17.9 %collective-permute-start.42 = (f32[3,34]{1,0:T(4,128)S(1)}, f32[3,34]{1,0:T(4,128)S(1)}, u32[]{:S(2)}, u32[]{:S(2)}) collective-permute-start(f32[3,34]{1,0:T(4,128)S(1)} %bitcast.1479), channel_id=1, source_target_pairs={{510,0},{511,1},{0,2},{1,3},{2,4},{3,5},{4,6},{5,7},{6,8},{7,9},{8... | collective-permute-start | bytes 1232 | tf_op jit(solution)/shard_map/ppermute | solution.py:16
  1138.9 19.7 %collective-permute-start.43 = (f32[3,34]{1,0:T(4,128)S(1)}, f32[3,34]{1,0:T(4,128)S(1)}, u32[]{:S(2)}, u32[]{:S(2)}) collective-permute-start(f32[3,34]{1,0:T(4,128)S(1)} %bitcast.1470), channel_id=1, source_target_pairs={{511,0},{0,1},{1,2},{2,3},{3,4},{4,5},{5,6},{6,7},{7,8},{8,9},{9,1... | collective-permute-start | bytes 1232 | tf_op jit(solution)/shard_map/ppermute | solution.py:16
  1141.0 17.6 %collective-permute-start.44 = (f32[3,34]{1,0:T(4,128)S(1)}, f32[3,34]{1,0:T(4,128)S(1)}, u32[]{:S(2)}, u32[]{:S(2)}) collective-permute-start(f32[3,34]{1,0:T(4,128)S(1)} %bitcast.1464), channel_id=1, source_target_pairs={{1,0},{2,1},{3,2},{4,3},{5,4},{6,5},{7,6},{8,7},{9,8},{10,9},{11,1... | collective-permute-start | bytes 1232 | tf_op jit(solution)/shard_map/ppermute | solution.py:16
  1143.5 15.1 %collective-permute-start.45 = (f32[3,34]{1,0:T(4,128)S(1)}, f32[3,34]{1,0:T(4,128)S(1)}, u32[]{:S(2)}, u32[]{:S(2)}) collective-permute-start(f32[3,34]{1,0:T(4,128)S(1)} %bitcast.1459), channel_id=1, source_target_pairs={{2,0},{3,1},{4,2},{5,3},{6,4},{7,5},{8,6},{9,7},{10,8},{11,9},{12,... | collective-permute-start | bytes 1232 | tf_op jit(solution)/shard_map/ppermute | solution.py:16
  1152.0 6.7 collective-permute-start.46
  1154.6 5.2 collective-permute-start.47
  (2 other events, 13.6 us)
where the time goes:
time: 1270 us; the launch traced here: 1260 us
  blocking collectives  866 us (68%)
  starting transfers between devices  187 us (15%)
  other arithmetic  133 us (10%)
  local copies, waits for them, and re-layouts  52.8 us (4%)
  between operations  15.2 us (1%)
    psum x5, blocking collectives, squares_sum(): return lax.psum(local_inner(field, field), 'parts')  476 us
    psum x4, blocking collectives, shards(): step_size = norm_now / lax.psum(local_inner(direction, image), 'parts')  390 us
    ppermute x48, starting transfers between devices, shifted(): return lax.ppermute(block, axis, route)  187 us
    scatter-add x5, other arithmetic, apply_local(): summed.at[:, element_nodes].add(jnp.transpose(element_terms, (1, 0, 2)))  101 us
    gather x10, local copies, waits for them, and re-layouts, apply_local(): element_values = jnp.take(field, element_nodes, axis=1)  31.8 us
  transfers between devices with their start and end apart: 48, of which 7 were waited for; matrix products, arithmetic and copies ran while one was open for 0% of the time, Pallas kernels for 0%

commit v1 on v0

v1 whole, which is shorter than its diff:
```python
import functools

import jax
import jax.numpy as jnp
import ml_dtypes
import numpy as np
from jax import lax
from jax.experimental import pallas as pl
from jax.experimental.pallas import tpu as pltpu
from jax.sharding import PartitionSpec as P

ITERS = 5
DAMPING = 2.0
MESH = pl.DeviceIdType.MESH
F32 = jnp.float32
BF16 = jnp.bfloat16

NODES = 1445
NODE_ROWS = 12
ROWS = 24
PEERS = 8
SHARE = 34
SHIFT_SCALE = 0.045


def shape_table():
    points = np.array([-np.sqrt(0.6), 0.0, np.sqrt(0.6)])
    values = np.stack(
        [points * (points - 1.0) / 2.0, 1.0 - points * points, points * (points + 1.0) / 2.0],
        axis=1,
    )
    slopes = np.stack([points - 0.5, -2.0 * points, points + 0.5], axis=1)
    result = np.zeros((27, 3, 27))
    for direction in range(3):
        factors = [slopes if axis_index == direction else values for axis_index in range(3)]
        product = (
            factors[0][:, None, None, :, None, None]
            * factors[1][None, :, None, None, :, None]
            * factors[2][None, None, :, None, None, :]
        )
        result[:, direction, :] = product.reshape(27, 27)
    return result


def three_parts(table):
    rest = table.astype(np.float32)
    parts = []
    for _ in range(3):
        part = rest.astype(ml_dtypes.bfloat16)
        parts.append(part)
        rest = rest - part.astype(np.float32)
    return parts


def tables():
    table = shape_table()
    forward = np.zeros((3, 32, 32))
    forward[:, :27, :27] = table.transpose(1, 0, 2)
    high, mid, low = three_parts(forward.reshape(96, 32))
    first = np.concatenate([high, high, high, mid, mid, low], axis=1)
    weights = np.einsum("qda,qfa->dfq", table, table)
    row = np.zeros((16, 6, 32))
    for pair, (one, two) in enumerate(PAIRS):
        row[0, pair, :27] = weights[one, two] * (1.0 if one == two else 2.0)
    first = np.concatenate([first, row.reshape(16, 192).astype(ml_dtypes.bfloat16)], axis=0)
    high, mid, low = three_parts(forward.transpose(2, 0, 1).reshape(32, 96))
    zero = np.zeros_like(high)
    second = np.concatenate(
        [
            np.concatenate([high, high, high], axis=1),
            np.concatenate([mid, mid, zero], axis=1),
            np.concatenate([low, zero, zero], axis=1),
        ],
        axis=0,
    )
    return first, second


PAIRS = [(0, 0), (0, 1), (0, 2), (1, 1), (1, 2), (2, 2)]


def packed_index(row_index, col_index):
    first = min(row_index, col_index)
    second = max(row_index, col_index)
    return first * 9 - first * (first - 1) // 2 + (second - first)


def peer_offsets(count):
    half = count // 2
    return [offset - half for offset in range(half)] + [offset + 1 for offset in range(half)]


def stage_digits(count):
    if count == 512:
        return [[(1, 2), (2, 8)], [(16, 8), (128, 4)]]
    small = 1
    while small * small < count:
        small *= 2
    return [[(1, small)], [(small, count // small)]]


def partners(me, digits):
    size = int(np.prod([digit for _, digit in digits]))
    place, scale, base = 0, 1, me
    for stride, digit in digits:
        value = lax.rem(lax.div(me, stride), digit)
        place = place + value * scale
        scale *= digit
        base = base - value * stride
    result = []
    for step in range(1, size):
        other = lax.rem(place + step, size)
        number = base
        for stride, digit in digits:
            number = number + lax.rem(other, digit) * stride
            other = lax.div(other, digit)
        result.append(number)
    return result


def parts_of(value):
    high = value.astype(BF16).astype(F32)
    rest = value - high
    mid = rest.astype(BF16).astype(F32)
    return high, mid, (rest - mid).astype(BF16).astype(F32)


def lane_of(row, lane):
    return jnp.broadcast_to(row[:, lane : lane + 1], (1, 128))


def spread(ref, row):
    return jnp.broadcast_to(ref[pl.ds(row, 1), :], (8, 128))


def pick(ref, base, count, first, rows, lanes, start):
    result = start
    for row in range(count):
        found = jnp.take_along_axis(spread(ref, base + row), lanes, axis=1)
        result = jnp.where(rows == first + row, found, result)
    return result


def kernel(
    count,
    rhs_ref,
    conn_ref,
    hess_ref,
    shared_ref,
    owner_ref,
    first_ref,
    second_ref,
    out_ref,
    nodes_scr,
    owner_scr,
    shared_scr,
    map_scr,
    conn_scr,
    row_scr,
    lane_scr,
    hot_scr,
    h_scr,
    q_scr,
    own_scr,
    inner_scr,
    in_scr,
    part_scr,
    u_scr,
    g_scr,
    s_scr,
    t_scr,
    rs_scr,
    ri_scr,
    weight_scr,
    moment_scr,
    scale_scr,
    basis_scr,
    send_buf,
    recv_buf,
    sum_out,
    sum_in0,
    sum_in1,
    halo_send,
    halo_recv,
    sum_send,
    sum_recv,
):
    me = lax.axis_index("parts")
    peers = [lax.rem(me + offset + count, count) for offset in peer_offsets(PEERS)]
    stages = [partners(me, digits) for digits in stage_digits(count)]
    sum_in = [sum_in0, sum_in1]

    barrier = pltpu.get_barrier_semaphore()
    everyone = peers + stages[0] + stages[1]
    for other in everyone:
        pl.semaphore_signal(barrier, inc=1, device_id=(other,), device_id_type=MESH)

    sublane = lax.broadcasted_iota(jnp.int32, (8, 128), 0)
    lane = lax.broadcasted_iota(jnp.int32, (8, 128), 1)
    sublane16 = lax.broadcasted_iota(jnp.int32, (16, 128), 0)

    def send_halo(turn):
        for j in range(PEERS):
            pltpu.make_async_remote_copy(
                src_ref=send_buf.at[turn, j],
                dst_ref=recv_buf.at[turn, PEERS - 1 - j],
                send_sem=halo_send.at[turn],
                recv_sem=halo_recv.at[turn],
                device_id=(peers[j],),
                device_id_type=MESH,
            ).start()

    def wait_halo(turn):
        pltpu.make_async_copy(recv_buf.at[turn], recv_buf.at[turn], halo_recv.at[turn]).wait()

    def send_sum(which, stage, row):
        slot = 2 * which + stage
        sum_out[slot] = row
        for k, other in enumerate(stages[stage]):
            pltpu.make_async_remote_copy(
                src_ref=sum_out.at[slot],
                dst_ref=sum_in[stage].at[which, k],
                send_sem=sum_send.at[slot],
                recv_sem=sum_recv.at[slot],
                device_id=(other,),
                device_id_type=MESH,
            ).start()

    def wait_sum(which, stage):
        slot = 2 * which + stage
        arrived = sum_in[stage].at[which]
        pltpu.make_async_copy(arrived, arrived, sum_recv.at[slot]).wait()
        terms = [sum_out[slot]] + [sum_in[stage][which, k] for k in range(len(stages[stage]))]
        while len(terms) > 1:
            terms = [sum(terms[i : i + 2]) for i in range(0, len(terms), 2)]
        return terms[0]

    nodes_scr[...] = jnp.zeros_like(nodes_scr)
    owner_scr[...] = jnp.zeros_like(owner_scr)
    for r in range(NODE_ROWS):
        width = min(128, NODES - 128 * r)
        for c in range(3):
            nodes_scr[pl.ds(16 * c + r, 1), 0:width] = rhs_ref[c : c + 1, 128 * r : 128 * r + width]
        owner_scr[pl.ds(r, 1), 0:width] = owner_ref[0:1, 128 * r : 128 * r + width].astype(F32)
    shared_scr[...] = jnp.full((8, 128), NODES, jnp.int32)
    shared_scr[:, 0:SHARE] = shared_ref[...]
    names = shared_scr[...]
    used = names < NODES
    name_rows, name_lanes = names >> 7, names & 127
    zero = jnp.zeros((8, 128), F32)
    for c in range(3):
        found = pick(nodes_scr, 16 * c, NODE_ROWS, 0, name_rows, name_lanes, zero)
        own_scr[pl.ds(8 * c, 8), :] = jnp.where(used, found, 0.0)
    weight_scr[0:8, :] = jnp.where(
        used, pick(owner_scr, 0, NODE_ROWS, 0, name_rows, name_lanes, zero), 0.0
    )

    def fill_message(turn):
        for c in range(3):
            for j in range(PEERS):
                send_buf[turn, j, c] = own_scr[pl.ds(8 * c + j, 1), :]

    fill_message(0)
    pl.semaphore_wait(barrier, len(everyone))
    send_halo(0)

    for k in range(45):
        h_scr[k, 24:32, :] = jnp.zeros((8, 128), F32)
        h_scr[k, 0:27, :] = hess_ref[k].astype(F32)
    sums = []
    for one, two in PAIRS:
        total = h_scr[packed_index(one, two)]
        for i in range(1, 3):
            total = total + h_scr[packed_index(3 * i + one, 3 * i + two)]
        sums.append(total)
    stacked = jnp.concatenate(sums, axis=0).astype(BF16)
    traces = jnp.dot(first_ref[96:112, :], stacked, preferred_element_type=F32)[0:1, :]

    def row_of(values):
        totals = jnp.sum(values, axis=1, keepdims=True)
        rows = lax.broadcasted_iota(jnp.int32, values.shape, 0)
        lanes = lax.broadcasted_iota(jnp.int32, values.shape, 1)
        return jnp.sum(jnp.where(rows == lanes, totals, 0.0), axis=0, keepdims=True)

    both = jnp.where(sublane == 0, traces, jnp.where(sublane == 1, traces * traces, 0.0))
    send_sum(0, 0, row_of(both))

    found = jnp.zeros((32, 128), F32)
    for j in range(PEERS):
        rows_j = jnp.broadcast_to(jnp.where(used, name_rows, 99)[j : j + 1, :], (16, 128))
        lanes_j = jnp.broadcast_to(name_lanes[j : j + 1, :], (128, 128))
        hit = rows_j == sublane16
        slot = lax.broadcasted_iota(jnp.int32, (16, 128), 1).astype(F32)
        left = jnp.concatenate(
            [jnp.where(hit, float(j + 1), 0.0), jnp.where(hit, slot, 0.0)], axis=0
        )
        right = jnp.where(
            lanes_j == lax.broadcasted_iota(jnp.int32, (128, 128), 0), 1.0, 0.0
        )
        found = found + lax.dot_general(
            left.astype(BF16),
            right.astype(BF16),
            (((1,), (1,)), ((), ())),
            preferred_element_type=F32,
        )
    map_scr[...] = (64.0 * found[0:16] + found[16:32]).astype(jnp.int32)
    weight_scr[8:24, :] = jnp.where(map_scr[...] > 0, 0.0, owner_scr[...])

    conn_scr[...] = jnp.zeros_like(conn_scr)
    conn_scr[0:27, :] = conn_ref[...]
    for t in range(4):
        names_t = conn_scr[pl.ds(8 * t, 8), :]
        rows_t, lanes_t = names_t >> 7, names_t & 127
        where_t = pick(map_scr, 0, NODE_ROWS, 0, rows_t, lanes_t, jnp.zeros((8, 128), jnp.int32))
        is_shared = where_t > 0
        row_t = jnp.where(is_shared, (where_t >> 6) - 1, rows_t + 8)
        if t == 3:
            row_t = jnp.where(sublane < 3, row_t, 99)
        row_scr[pl.ds(8 * t, 8), :] = row_t
        lane_scr[pl.ds(8 * t, 8), :] = jnp.where(is_shared, where_t & 63, lanes_t)

    columns = jnp.transpose(lane_scr[...].astype(F32))
    lanes_all = lax.broadcasted_iota(jnp.int32, (128, 128), 1).astype(F32)
    for a in range(27):
        column = jnp.broadcast_to(columns[:, a : a + 1], (128, 128))
        hot_scr[pl.ds(128 * a, 128), :] = jnp.where(column == lanes_all, 1.0, 0.0).astype(BF16)

    for c in range(3):
        q_scr[0, pl.ds(24 * c + 8, 16), :] = jnp.where(
            map_scr[...] > 0, 0.0, nodes_scr[pl.ds(16 * c, 16), :]
        )
    moment_scr[...] = jnp.zeros_like(moment_scr)

    def gather_inner(turn):
        for t in range(4):
            rows_t = row_scr[pl.ds(8 * t, 8), :]
            lanes_t = lane_scr[pl.ds(8 * t, 8), :]
            for c in range(3):
                part_scr[pl.ds(8 * t, 8), 128 * c : 128 * c + 128] = pick(
                    q_scr.at[turn], 24 * c + 8, NODE_ROWS, 8, rows_t, lanes_t, zero
                )

    gather_inner(0)
    send_sum(0, 1, wait_sum(0, 0))

    def moment(index, one, two):
        total = zero
        for c in range(3):
            for t in range(3):
                rows = pl.ds(24 * c + 8 * t, 8)
                total = total + weight_scr[pl.ds(8 * t, 8), :] * q_scr[one, rows, :] * q_scr[two, rows, :]
        moment_scr[pl.ds(index, 1), :] = jnp.sum(total, axis=0, keepdims=True)

    def write_basis(turn):
        for t in range(2):
            where_t = map_scr[pl.ds(8 * t, 8), :]
            rows_t, lanes_t = (where_t >> 6) - 1, where_t & 63
            for c in range(3):
                inner = q_scr[turn, pl.ds(24 * c + 8 + 8 * t, 8), :]
                value = pick(q_scr.at[turn], 24 * c, 8, 0, rows_t, lanes_t, inner)
                for r in range(8 if t == 0 else 4):
                    basis_scr[turn, pl.ds(c, 1), 128 * (8 * t + r) : 128 * (8 * t + r) + 128] = (
                        value[r : r + 1, :]
                    )

    def receive(turn, is_first):
        wait_halo(turn)
        for c in range(3):
            for j in range(PEERS):
                in_scr[pl.ds(8 * c + j, 1), :] = recv_buf[turn, j, c]
        for c in range(3):
            value = own_scr[pl.ds(8 * c, 8), :] + in_scr[pl.ds(8 * c, 8), :]
            if not is_first:
                before = q_scr[turn - 1, pl.ds(24 * c, 8), :]
                scale = spread(scale_scr, 0)
                value = value * scale + before * (DAMPING * scale - 1.0)
            q_scr[turn, pl.ds(24 * c, 8), :] = value

    def stresses(turn):
        for t in range(4):
            rows_t = row_scr[pl.ds(8 * t, 8), :]
            lanes_t = lane_scr[pl.ds(8 * t, 8), :]
            for c in range(3):
                u_scr[pl.ds(8 * t, 8), 128 * c : 128 * c + 128] = pick(
                    q_scr.at[turn],
                    24 * c,
                    8,
                    0,
                    rows_t,
                    lanes_t,
                    part_scr[pl.ds(8 * t, 8), 128 * c : 128 * c + 128],
                )
        high, mid, low = parts_of(u_scr[...])
        right = jnp.concatenate([high, mid, low, high, mid, high], axis=0).astype(BF16)
        g_scr[...] = jnp.dot(first_ref[0:96, :], right, preferred_element_type=F32)
        energy = zero
        for t in range(2):
            grads = [
                g_scr[32 * (n % 3) + 16 * t : 32 * (n % 3) + 16 * t + 16, 128 * (n // 3) : 128 * (n // 3) + 128]
                for n in range(9)
            ]
            for m in range(9):
                total = h_scr[packed_index(m, 0), pl.ds(16 * t, 16), :] * grads[0]
                for n in range(1, 9):
                    total = total + h_scr[packed_index(m, n), pl.ds(16 * t, 16), :] * grads[n]
                product = total * grads[m]
                energy = energy + product[0:8] + product[8:16]
                for p, part in enumerate(parts_of(total)):
                    row = 96 * p + 32 * (m % 3) + 16 * t
                    s_scr[row : row + 16, 128 * (m // 3) : 128 * (m // 3) + 128] = part.astype(BF16)
        return energy

    def terms():
        blocks = jnp.dot(second_ref[...], s_scr[...], preferred_element_type=F32)
        summed = blocks[0:32] + blocks[32:64] + blocks[64:96]
        for p, part in enumerate(parts_of(summed)):
            t_scr[p] = part

    def scatter(target, first, height):
        numbers = lax.broadcasted_iota(jnp.int32, (height, 128), 0) + first
        for a in range(27):
            mask = jnp.broadcast_to(row_scr[pl.ds(a, 1), :], (height, 128)) == numbers
            groups = [
                jnp.where(
                    mask,
                    jnp.broadcast_to(t_scr[p, pl.ds(a, 1), 128 * c : 128 * c + 128], (height, 128)),
                    0.0,
                )
                for c in range(3)
                for p in range(3)
            ]
            if height == 8:
                groups.append(jnp.zeros((8, 128), F32))
                groups = [
                    jnp.concatenate(groups[i : i + 2], axis=0) for i in range(0, len(groups), 2)
                ]
            for i, group in enumerate(groups):
                target[16 * i : 16 * i + 16, 128 * a : 128 * a + 128] = group.astype(BF16)
        summed = jnp.dot(target[...], hot_scr[...], preferred_element_type=F32)
        return [
            summed[3 * height * c : 3 * height * c + height]
            + summed[3 * height * c + height : 3 * height * c + 2 * height]
            + summed[3 * height * c + 2 * height : 3 * height * c + 3 * height]
            for c in range(3)
        ]

    def scatter_shared(turn):
        for c, value in enumerate(scatter(rs_scr, 0, 8)):
            own_scr[pl.ds(8 * c, 8), :] = value
        fill_message(turn + 1)
        send_halo(turn + 1)

    def inner_rows(turn):
        scale = jnp.broadcast_to(scale_scr[0:1, :], (16, 128))
        for c in range(3):
            rows = pl.ds(24 * c + 8, 16)
            q_scr[turn + 1, rows, :] = inner_scr[pl.ds(16 * c, 16), :] * scale + q_scr[
                turn, rows, :
            ] * (DAMPING * scale - 1.0)

    def scatter_inner():
        for c, value in enumerate(scatter(ri_scr, 8, 16)):
            inner_scr[pl.ds(16 * c, 16), :] = value

    def turn_of(turn, is_first):
        receive(turn, is_first)
        stresses(turn)
        terms()
        scatter_shared(turn)
        scatter_inner()
        moment(2 * turn, turn, turn)
        if is_first:
            write_basis(turn)
            row = wait_sum(0, 1)
            total, squares = lane_of(row, 0), lane_of(row, 1)
            scale_scr[0:1, :] = 1.0 / (DAMPING + SHIFT_SCALE * squares / total)
            inner_rows(turn)
            gather_inner(turn + 1)
        else:
            inner_rows(turn)
            gather_inner(turn + 1)
            moment(2 * turn - 1, turn - 1, turn)
            write_basis(turn)

    turn_of(0, True)

    def body(turn, carry):
        turn_of(turn, False)
        return carry

    lax.fori_loop(1, ITERS - 1, body, 0)

    last = ITERS - 1
    receive(last, False)
    moment(2 * last - 1, last - 1, last)
    moment(2 * last, last, last)
    energy = stresses(last)
    moment_scr[pl.ds(2 * last + 1, 1), :] = jnp.sum(energy, axis=0, keepdims=True)
    send_sum(1, 0, row_of(moment_scr[...]))
    terms()
    scatter_shared(last)
    scatter_inner()
    send_sum(1, 1, wait_sum(1, 0))
    inner_rows(last)
    write_basis(last)
    receive(ITERS, False)
    write_basis(ITERS)
    row = wait_sum(1, 1)

    scale = scale_scr[0:1, :]
    m = [lane_of(row, k) for k in range(2 * ITERS)]
    m[2 * last + 1] = m[2 * last + 1] * scale + m[2 * last] * (DAMPING * scale - 1.0)
    low = [[None] * ITERS for _ in range(ITERS)]
    low_d = [[None] * ITERS for _ in range(ITERS)]
    inverse = [None] * ITERS
    right = [None] * ITERS
    for j in range(ITERS):
        pivot = m[2 * j]
        value = m[j + ITERS]
        for k in range(j):
            pivot = pivot - low[j][k] * low_d[j][k]
            value = value - low[j][k] * right[k]
        inverse[j] = 1.0 / pivot
        right[j] = value
        for i in range(j + 1, ITERS):
            entry = m[i + j]
            for k in range(j):
                entry = entry - low[i][k] * low_d[j][k]
            low_d[i][j] = entry
            low[i][j] = entry * inverse[j]
    coef = [None] * ITERS
    for i in reversed(range(ITERS)):
        value = right[i] * inverse[i]
        for k in range(i + 1, ITERS):
            value = value - low[k][i] * coef[k]
        coef[i] = value
    norm = -1.0
    for i in range(ITERS):
        norm = norm - coef[i] if i % 2 == 0 else norm + coef[i]
    by_norm = 1.0 / norm
    rest = [-value * by_norm for value in coef] + [by_norm]
    steps = [1.0 - rest[0]]
    for i in range(1, ITERS):
        steps.append(-rest[i] - steps[-1])
    rest = [jnp.broadcast_to(value, (8, 128)) for value in rest]
    steps = [jnp.broadcast_to(value * scale, (8, 128)) for value in steps]
    for r in range(NODE_ROWS):
        width = min(128, NODES - 128 * r)
        tiles = [basis_scr[i, :, 128 * r : 128 * r + 128] for i in range(ITERS + 1)]
        newton = tiles[0] * steps[0]
        for i in range(1, ITERS):
            newton = newton + tiles[i] * steps[i]
        left = tiles[0] * rest[0]
        for i in range(1, ITERS + 1):
            left = left + tiles[i] * rest[i]
        out_ref[0, :, 128 * r : 128 * r + width] = newton[0:3, 0:width]
        out_ref[1, :, 128 * r : 128 * r + width] = left[0:3, 0:width]

    for turn in range(ITERS + 1):
        pltpu.make_async_copy(send_buf.at[turn], send_buf.at[turn], halo_send.at[turn]).wait()
    for which in range(2):
        for stage in range(2):
            arrived = sum_in[stage].at[which]
            pltpu.make_async_copy(arrived, arrived, sum_send.at[2 * which + stage]).wait()


def shards(count, rhs_partial, connectivity, hessians, shared_nodes, owner):
    first, second = tables()
    sizes = [int(np.prod([d for _, d in digits])) - 1 for digits in stage_digits(count)]
    vmem = pltpu.VMEM
    out = pl.pallas_call(
        functools.partial(kernel, count),
        out_shape=jax.ShapeDtypeStruct((2, 3, NODES), F32),
        in_specs=[pl.BlockSpec(memory_space=vmem)] * 7,
        out_specs=pl.BlockSpec(memory_space=vmem),
        scratch_shapes=[
            vmem((48, 128), F32),
            vmem((16, 128), F32),
            vmem((8, 128), jnp.int32),
            vmem((16, 128), jnp.int32),
            vmem((32, 128), jnp.int32),
            vmem((32, 128), jnp.int32),
            vmem((32, 128), jnp.int32),
            vmem((27 * 128, 128), BF16),
            vmem((45, 32, 128), F32),
            vmem((ITERS + 1, 3 * ROWS, 128), F32),
            vmem((24, 128), F32),
            vmem((48, 128), F32),
            vmem((24, 128), F32),
            vmem((32, 384), F32),
            vmem((32, 384), F32),
            vmem((96, 384), F32),
            vmem((288, 384), BF16),
            vmem((3, 32, 384), F32),
            vmem((80, 27 * 128), BF16),
            vmem((144, 27 * 128), BF16),
            vmem((ROWS, 128), F32),
            vmem((16, 128), F32),
            vmem((8, 128), F32),
            vmem((ITERS + 1, 8, NODE_ROWS * 128), F32),
            vmem((ITERS + 1, PEERS, 3, 1, 128), F32),
            vmem((ITERS + 1, PEERS, 3, 1, 128), F32),
            vmem((4, 1, 128), F32),
            vmem((2, sizes[0], 1, 128), F32),
            vmem((2, sizes[1], 1, 128), F32),
            pltpu.SemaphoreType.DMA((ITERS + 1,)),
            pltpu.SemaphoreType.DMA((ITERS + 1,)),
            pltpu.SemaphoreType.DMA((4,)),
            pltpu.SemaphoreType.DMA((4,)),
        ],
        compiler_params=pltpu.CompilerParams(
            collective_id=0, has_side_effects=True, vmem_limit_bytes=32 * 1024 * 1024
        ),
        name="newton_cg",
    )(
        rhs_partial,
        connectivity,
        hessians,
        shared_nodes,
        owner.reshape(1, NODES),
        jnp.asarray(first),
        jnp.asarray(second),
    )
    return out[0], out[1]


def solution(mesh):
    in_specs = (
        P(None, "parts"),
        P(None, "parts"),
        P(None, None, "parts"),
        P(None, "parts"),
        P("parts"),
    )
    out_specs = (P(None, "parts"), P(None, "parts"))
    return jax.shard_map(
        functools.partial(shards, mesh.shape["parts"]),
        mesh=mesh,
        in_specs=in_specs,
        out_specs=out_specs,
        check_vma=False,
    )
```

time: 1270 us -> 61.2 us (0.05)
  blocking collectives: 866 us -> 0 us
  starting transfers between devices: 187 us -> 0 us
  other arithmetic: 133 us -> 0 us
  Pallas kernels: 0 us -> 57.8 us
  local copies, waits for them, and re-layouts: 52.8 us -> 2.48 us
  between operations: 15.2 us -> 0.71 us
    psum x9 -> x0, blocking collectives: 866 us -> none  [the longest x5 476 us: squares_sum(): return lax.psum(local_inner(field, field), 'parts')]
    ppermute x48 -> x0, starting transfers between devices: 187 us -> none  [shifted(): return lax.ppermute(block, axis, route)]
    scatter-add x11 -> x0, other arithmetic: 115 us -> none  [the longest x5 101 us: apply_local(): summed.at[:, element_nodes].add(jnp.transpose(element_terms, (1, 0, 2)))]
    pallas_call x0 -> x1, Pallas kernels: none -> 57.8 us  [shards(): pl.pallas_call(functools.partial(kernel, count), out_shape=jax.ShapeDtype...]
    gather x28 -> x0, local copies, waits for them, and re-layouts: 39.1 us -> none  [the longest x10 31.8 us: apply_local(): element_values = jnp.take(field, element_nodes, axis=1)]
  transfers between devices with their start and end apart: 48 -> 0, of which waited for: 7 -> 0; matrix products, arithmetic and copies ran while one was open for 0% -> 0% of each run, Pallas kernels for 0% -> 0%
where the time goes in v1:
time: 61.2 us; the launch traced here: 61 us
  Pallas kernels  57.8 us (94%)
  local copies, waits for them, and re-layouts  2.48 us (4%)
  between operations  0.71 us (1%)
    pallas_call x1, Pallas kernels, shards(): pl.pallas_call(functools.partial(kernel, count), out_shape=jax.ShapeDtype...  57.8 us

profile of v1, /device:TPU:1, one launch (start us, length us, event | category | flops | bytes accessed | tf_op | source)
XLA Modules:
  0.0 61.0 jit_solution(12120447478057039228)
XLA Ops:
  0.6 0.7 %reshape.7.owner_ref = s32[1,1445]{1,0:T(1,128)S(1)} reshape(s32[1445]{0:T(1024)} %param.11) | data formatting | bytes 11560 | tf_op jit(solution)/shard_map/reshape | solution.py:620
  1.3 0.0 copy-start
  1.3 0.0 copy-start.1
  1.3 0.0 copy-start.2
  1.4 0.0 copy-start.3
  1.4 0.0 copy-start.4
  1.4 1.1 %copy.9.hess_ref = bf16[45,27,128]{2,1,0:T(8,128)(2,1)S(1)} copy(bf16[45,27,128]{2,0,1:T(8,128)(2,1)} %param.9) | data formatting | bytes 622080 | tf_op args[2]
  2.5 0.0 copy-done
  2.5 0.0 copy-done.1
  2.5 0.0 copy-done.2
  2.5 0.0 copy-done.3
  2.5 0.0 copy-done.4
  2.6 57.8 %newton_cg.1 = f32[2,3,1445]{2,1,0:T(4,128)S(1)} custom-call(f32[3,1445]{1,0:T(4,128)S(1)} %copy-done.2, s32[27,128]{1,0:T(8,128)S(1)} %copy-done.3, bf16[45,27,128]{2,1,0:T(8,128)(2,1)S(1)} %copy.9.hess_ref, s32[8,34]{1,0:T(8,128)S(1)} %copy-done.4, s32[1,1445]{1,0:T(1,128)S(1)} %reshape.7.owner_ref, bf16[112,192]{1,0:T(8,128)(2,1)S(1)} %copy-done.1, ...), custom_call_target="tpu_custom_call" | custom-call | tf_op jit(solution)/shard_map/newton_cg/pallas_call | solution.py:571
  60.4 0.6 %slice_bitcast_fusion = (f32[3,1445]{1,0:T(4,128)}, f32[3,1445]{1,0:T(4,128)}) fusion(f32[2,3,1445]{2,1,0:T(4,128)S(1)} %newton_cg.1), kind=kLoop, calls=%fused_computation | loop fusion | bytes 69360 | tf_op jit(solution)/shard_map/squeeze | solution.py:624
Async XLA Ops:
  1.3 1.2 %copy-start = (bf16[96,288]{1,0:T(8,128)(2,1)S(1)}, bf16[96,288]{1,0:T(8,128)(2,1)}, u32[]{:S(2)}) copy-start(bf16[96,288]{1,0:T(8,128)(2,1)} %constant.5.clone.second_ref) | copy-start | bytes 165892
  1.3 1.2 %copy-start.1 = (bf16[112,192]{1,0:T(8,128)(2,1)S(1)}, bf16[112,192]{1,0:T(8,128)(2,1)}, u32[]{:S(2)}) copy-start(bf16[112,192]{1,0:T(8,128)(2,1)} %constant.4.clone.first_ref) | copy-start | bytes 129028
  1.3 1.2 %copy-start.2 = (f32[3,1445]{1,0:T(4,128)S(1)}, f32[3,1445]{1,0:T(4,128)}, u32[]{:S(2)}) copy-start(f32[3,1445]{1,0:T(4,128)} %rhs_ref.1) | copy-start | bytes 52024
  1.4 1.2 %copy-start.3 = (s32[27,128]{1,0:T(8,128)S(1)}, s32[27,128]{1,0:T(8,128)}, u32[]{:S(2)}) copy-start(s32[27,128]{1,0:T(8,128)} %conn_ref.1) | copy-start | bytes 41476
  1.4 1.2 %copy-start.4 = (s32[8,34]{1,0:T(8,128)S(1)}, s32[8,34]{1,0:T(8,128)}, u32[]{:S(2)}) copy-start(s32[8,34]{1,0:T(8,128)} %shared_ref.1) | copy-start | bytes 3268

commit v2 on v1

--- a/solution.py
+++ b/solution.py
@@ -143,6 +143,14 @@
 
 def kernel(
     count,
+    rhs_hbm,
+    conn_hbm,
+    hess_hbm,
+    shared_hbm,
+    owner_hbm,
+    first_hbm,
+    second_hbm,
+    out_ref,
     rhs_ref,
     conn_ref,
     hess_ref,
@@ -150,7 +158,7 @@
     owner_ref,
     first_ref,
     second_ref,
-    out_ref,
+    load_sem,
     nodes_scr,
     owner_scr,
     shared_scr,
@@ -159,6 +167,7 @@
     row_scr,
     lane_scr,
     hot_scr,
+    wide_scr,
     h_scr,
     q_scr,
     own_scr,
@@ -195,6 +204,23 @@
     for other in everyone:
         pl.semaphore_signal(barrier, inc=1, device_id=(other,), device_id_type=MESH)
 
+    loads = [
+        pltpu.make_async_copy(source, target, load_sem.at[i])
+        for i, (source, target) in enumerate(
+            [
+                (rhs_hbm, rhs_ref),
+                (shared_hbm, shared_ref),
+                (owner_hbm, owner_ref),
+                (hess_hbm, hess_ref),
+                (first_hbm, first_ref),
+                (conn_hbm, conn_ref),
+                (second_hbm, second_ref),
+            ]
+        )
+    ]
+    for load in loads:
+        load.start()
+
     sublane = lax.broadcasted_iota(jnp.int32, (8, 128), 0)
     lane = lax.broadcasted_iota(jnp.int32, (8, 128), 1)
     sublane16 = lax.broadcasted_iota(jnp.int32, (16, 128), 0)
@@ -237,11 +263,13 @@
 
     nodes_scr[...] = jnp.zeros_like(nodes_scr)
     owner_scr[...] = jnp.zeros_like(owner_scr)
+    for load in loads[0:3]:
+        load.wait()
     for r in range(NODE_ROWS):
         width = min(128, NODES - 128 * r)
         for c in range(3):
             nodes_scr[pl.ds(16 * c + r, 1), 0:width] = rhs_ref[c : c + 1, 128 * r : 128 * r + width]
-        owner_scr[pl.ds(r, 1), 0:width] = owner_ref[0:1, 128 * r : 128 * r + width].astype(F32)
+        owner_scr[pl.ds(r, 1), 0:width] = owner_ref[128 * r : 128 * r + width].reshape(1, width).astype(F32)
     shared_scr[...] = jnp.full((8, 128), NODES, jnp.int32)
     shared_scr[:, 0:SHARE] = shared_ref[...]
     names = shared_scr[...]
@@ -264,9 +292,14 @@
     pl.semaphore_wait(barrier, len(everyone))
     send_halo(0)
 
+    for load in loads[3:]:
+        load.wait()
+    for q in range(27):
+        wide_scr[48 * q : 48 * q + 45, :] = hess_ref[q].astype(F32)
+    wide_scr[48 * 27 :, :] = jnp.zeros((48 * 5, 128), F32)
     for k in range(45):
-        h_scr[k, 24:32, :] = jnp.zeros((8, 128), F32)
-        h_scr[k, 0:27, :] = hess_ref[k].astype(F32)
+        for t in range(4):
+            h_scr[k, 8 * t : 8 * t + 8, :] = wide_scr[pl.ds(48 * 8 * t + k, 8, stride=48), :]
     sums = []
     for one, two in PAIRS:
         total = h_scr[packed_index(one, two)]
@@ -570,10 +603,18 @@
     vmem = pltpu.VMEM
     out = pl.pallas_call(
         functools.partial(kernel, count),
-        out_shape=jax.ShapeDtypeStruct((2, 3, NODES), F32),
-        in_specs=[pl.BlockSpec(memory_space=vmem)] * 7,
+        out_shape=vmem((2, 3, NODES), F32),
+        in_specs=[pl.BlockSpec(memory_space=pltpu.HBM)] * 7,
         out_specs=pl.BlockSpec(memory_space=vmem),
         scratch_shapes=[
+            vmem((3, NODES), F32),
+            vmem((27, 128), jnp.int32),
+            vmem((27, 45, 128), BF16),
+            vmem((8, SHARE), jnp.int32),
+            vmem((NODES,), jnp.int32),
+            vmem(first.shape, BF16),
+            vmem(second.shape, BF16),
+            pltpu.SemaphoreType.DMA((7,)),
             vmem((48, 128), F32),
             vmem((16, 128), F32),
             vmem((8, 128), jnp.int32),
@@ -582,6 +623,7 @@
             vmem((32, 128), jnp.int32),
             vmem((32, 128), jnp.int32),
             vmem((27 * 128, 128), BF16),
+            vmem((48 * 32, 128), F32),
             vmem((45, 32, 128), F32),
             vmem((ITERS + 1, 3 * ROWS, 128), F32),
             vmem((24, 128), F32),
@@ -608,16 +650,14 @@
             pltpu.SemaphoreType.DMA((4,)),
             pltpu.SemaphoreType.DMA((4,)),
         ],
-        compiler_params=pltpu.CompilerParams(
-            collective_id=0, has_side_effects=True, vmem_limit_bytes=32 * 1024 * 1024
-        ),
+        compiler_params=pltpu.CompilerParams(collective_id=0, has_side_effects=True),
         name="newton_cg",
     )(
         rhs_partial,
         connectivity,
-        hessians,
+        jnp.transpose(hessians, (1, 0, 2)),
         shared_nodes,
-        owner.reshape(1, NODES),
+        owner,
         jnp.asarray(first),
         jnp.asarray(second),
     )

time: 61.2 us -> 59.3 us (0.969)
  local copies, waits for them, and re-layouts: 2.48 us -> 0.62 us
    unnamed x11 -> x0, local copies, waits for them, and re-layouts: 1.16 us -> none
    reshape x1 -> x0, local copies, waits for them, and re-layouts: 0.7 us -> none  [shards(): owner.reshape(1, NODES)]
where the time goes in v2:
time: 59.3 us; the launch traced here: 59.1 us
  Pallas kernels  57.9 us (98%)
  between operations  0.64 us (1%)
  local copies, waits for them, and re-layouts  0.62 us (1%)
    pallas_call x1, Pallas kernels, shards(): pl.pallas_call(functools.partial(kernel, count), out_shape=vmem((2, 3, NO...  57.9 us

profile of v2, /device:TPU:1, one launch (start us, length us, event | category | flops | bytes accessed | tf_op | source)
XLA Modules:
  0.0 59.1 jit_solution(6842704057425976020)
XLA Ops:
  0.6 57.9 %newton_cg.1 = f32[2,3,1445]{2,1,0:T(4,128)S(1)} custom-call(f32[3,1445]{1,0:T(4,128)} %rhs_hbm.1, s32[27,128]{1,0:T(8,128)} %conn_hbm.1, bf16[27,45,128]{2,1,0:T(8,128)(2,1)} %bitcast.5, s32[8,34]{1,0:T(8,128)} %shared_hbm.1, s32[1445]{0:T(1024)} %owner_hbm.1, bf16[112,192]{1,0:T(8,128)(2,1)} %constant.4.clone.first_hbm, ...), custom_call_target="tpu_custom_call" | custom-call | tf_op jit(solution)/shard_map/newton_cg/pallas_call | solution.py:604
  58.5 0.6 %slice_bitcast_fusion = (f32[3,1445]{1,0:T(4,128)}, f32[3,1445]{1,0:T(4,128)}) fusion(f32[2,3,1445]{2,1,0:T(4,128)S(1)} %newton_cg.1), kind=kLoop, calls=%fused_computation | loop fusion | bytes 69360 | tf_op jit(solution)/shard_map/squeeze | solution.py:664

commit v3 on v2

--- a/solution.py
+++ b/solution.py
@@ -17,9 +17,12 @@
 
 NODES = 1445
 NODE_ROWS = 12
-ROWS = 24
+BASE = 4
+ROWS = BASE + NODE_ROWS
 PEERS = 8
 SHARE = 34
+PEER_ROW = [0, 0, 0, 2, 3, 1, 1, 1]
+PEER_LANE = [0, 40, 80, 0, 0, 80, 40, 0]
 SHIFT_SCALE = 0.045
 
 
@@ -90,32 +93,10 @@
     return [offset - half for offset in range(half)] + [offset + 1 for offset in range(half)]
 
 
-def stage_digits(count):
-    if count == 512:
-        return [[(1, 2), (2, 8)], [(16, 8), (128, 4)]]
-    small = 1
-    while small * small < count:
-        small *= 2
-    return [[(1, small)], [(small, count // small)]]
-
-
-def partners(me, digits):
-    size = int(np.prod([digit for _, digit in digits]))
-    place, scale, base = 0, 1, me
-    for stride, digit in digits:
-        value = lax.rem(lax.div(me, stride), digit)
-        place = place + value * scale
-        scale *= digit
-        base = base - value * stride
-    result = []
-    for step in range(1, size):
-        other = lax.rem(place + step, size)
-        number = base
-        for stride, digit in digits:
-            number = number + lax.rem(other, digit) * stride
-            other = lax.div(other, digit)
-        result.append(number)
-    return result
+def stage_masks(count):
+    bits = count.bit_length() - 1
+    low = 1 << min(4, bits - 1)
+    return [list(range(1, low)), [low * k for k in range(1, count // low)]]
 
 
 def parts_of(value):
@@ -178,8 +159,6 @@
     g_scr,
     s_scr,
     t_scr,
-    rs_scr,
-    ri_scr,
     weight_scr,
     moment_scr,
     scale_scr,
@@ -195,8 +174,8 @@
     sum_recv,
 ):
     me = lax.axis_index("parts")
-    peers = [lax.rem(me + offset + count, count) for offset in peer_offsets(PEERS)]
-    stages = [partners(me, digits) for digits in stage_digits(count)]
+    peers = [(me + offset) & (count - 1) for offset in peer_offsets(PEERS)]
+    stages = [[me ^ mask for mask in masks] for masks in stage_masks(count)]
     sum_in = [sum_in0, sum_in1]
 
     barrier = pltpu.get_barrier_semaphore()
@@ -228,7 +207,7 @@
     def send_halo(turn):
         for j in range(PEERS):
             pltpu.make_async_remote_copy(
-                src_ref=send_buf.at[turn, j],
+                src_ref=send_buf.at[turn, PEER_ROW[j]],
                 dst_ref=recv_buf.at[turn, PEERS - 1 - j],
                 send_sem=halo_send.at[turn],
                 recv_sem=halo_recv.at[turn],
@@ -268,25 +247,26 @@
     for r in range(NODE_ROWS):
         width = min(128, NODES - 128 * r)
         for c in range(3):
-            nodes_scr[pl.ds(16 * c + r, 1), 0:width] = rhs_ref[c : c + 1, 128 * r : 128 * r + width]
-        owner_scr[pl.ds(r, 1), 0:width] = owner_ref[128 * r : 128 * r + width].reshape(1, width).astype(F32)
+            nodes_scr[pl.ds(16 * c + BASE + r, 1), 0:width] = rhs_ref[c : c + 1, 128 * r : 128 * r + width]
+        owner_scr[pl.ds(BASE + r, 1), 0:width] = owner_ref[128 * r : 128 * r + width].reshape(1, width).astype(F32)
     shared_scr[...] = jnp.full((8, 128), NODES, jnp.int32)
-    shared_scr[:, 0:SHARE] = shared_ref[...]
+    for j in range(PEERS):
+        start = PEER_LANE[j]
+        shared_scr[PEER_ROW[j] : PEER_ROW[j] + 1, start : start + SHARE] = shared_ref[j : j + 1, :]
     names = shared_scr[...]
     used = names < NODES
-    name_rows, name_lanes = names >> 7, names & 127
+    name_rows, name_lanes = (names >> 7) + BASE, names & 127
     zero = jnp.zeros((8, 128), F32)
     for c in range(3):
-        found = pick(nodes_scr, 16 * c, NODE_ROWS, 0, name_rows, name_lanes, zero)
+        found = pick(nodes_scr, 16 * c + BASE, NODE_ROWS, BASE, name_rows, name_lanes, zero)
         own_scr[pl.ds(8 * c, 8), :] = jnp.where(used, found, 0.0)
-    weight_scr[0:8, :] = jnp.where(
-        used, pick(owner_scr, 0, NODE_ROWS, 0, name_rows, name_lanes, zero), 0.0
-    )
+    owned = pick(owner_scr, BASE, NODE_ROWS, BASE, name_rows, name_lanes, zero)
+    shared_weight = jnp.where(used, owned, 0.0)
 
     def fill_message(turn):
         for c in range(3):
-            for j in range(PEERS):
-                send_buf[turn, j, c] = own_scr[pl.ds(8 * c + j, 1), :]
+            for row in range(BASE):
+                send_buf[turn, row, c] = own_scr[pl.ds(8 * c + row, 1), :]
 
     fill_message(0)
     pl.semaphore_wait(barrier, len(everyone))
@@ -319,7 +299,7 @@
     send_sum(0, 0, row_of(both))
 
     found = jnp.zeros((32, 128), F32)
-    for j in range(PEERS):
+    for j in range(BASE):
         rows_j = jnp.broadcast_to(jnp.where(used, name_rows, 99)[j : j + 1, :], (16, 128))
         lanes_j = jnp.broadcast_to(name_lanes[j : j + 1, :], (128, 128))
         hit = rows_j == sublane16
@@ -336,21 +316,23 @@
             (((1,), (1,)), ((), ())),
             preferred_element_type=F32,
         )
-    map_scr[...] = (64.0 * found[0:16] + found[16:32]).astype(jnp.int32)
-    weight_scr[8:24, :] = jnp.where(map_scr[...] > 0, 0.0, owner_scr[...])
+    map_scr[...] = (128.0 * found[0:16] + found[16:32]).astype(jnp.int32)
+    others = jnp.where(map_scr[...] > 0, 0.0, owner_scr[...])
+    weight_scr[0:8, :] = others[0:8] + shared_weight
+    weight_scr[8:16, :] = others[8:16]
 
     conn_scr[...] = jnp.zeros_like(conn_scr)
     conn_scr[0:27, :] = conn_ref[...]
     for t in range(4):
         names_t = conn_scr[pl.ds(8 * t, 8), :]
-        rows_t, lanes_t = names_t >> 7, names_t & 127
-        where_t = pick(map_scr, 0, NODE_ROWS, 0, rows_t, lanes_t, jnp.zeros((8, 128), jnp.int32))
+        rows_t, lanes_t = (names_t >> 7) + BASE, names_t & 127
+        where_t = pick(map_scr, BASE, NODE_ROWS, BASE, rows_t, lanes_t, jnp.zeros((8, 128), jnp.int32))
         is_shared = where_t > 0
-        row_t = jnp.where(is_shared, (where_t >> 6) - 1, rows_t + 8)
+        row_t = jnp.where(is_shared, (where_t >> 7) - 1, rows_t)
         if t == 3:
             row_t = jnp.where(sublane < 3, row_t, 99)
         row_scr[pl.ds(8 * t, 8), :] = row_t
-        lane_scr[pl.ds(8 * t, 8), :] = jnp.where(is_shared, where_t & 63, lanes_t)
+        lane_scr[pl.ds(8 * t, 8), :] = jnp.where(is_shared, where_t & 127, lanes_t)
 
     columns = jnp.transpose(lane_scr[...].astype(F32))
     lanes_all = lax.broadcasted_iota(jnp.int32, (128, 128), 1).astype(F32)
@@ -359,7 +341,7 @@
         hot_scr[pl.ds(128 * a, 128), :] = jnp.where(column == lanes_all, 1.0, 0.0).astype(BF16)
 
     for c in range(3):
-        q_scr[0, pl.ds(24 * c + 8, 16), :] = jnp.where(
+        q_scr[0, pl.ds(16 * c, 16), :] = jnp.where(
             map_scr[...] > 0, 0.0, nodes_scr[pl.ds(16 * c, 16), :]
         )
     moment_scr[...] = jnp.zeros_like(moment_scr)
@@ -370,7 +352,7 @@
             lanes_t = lane_scr[pl.ds(8 * t, 8), :]
             for c in range(3):
                 part_scr[pl.ds(8 * t, 8), 128 * c : 128 * c + 128] = pick(
-                    q_scr.at[turn], 24 * c + 8, NODE_ROWS, 8, rows_t, lanes_t, zero
+                    q_scr.at[turn], 16 * c + BASE, NODE_ROWS, BASE, rows_t, lanes_t, zero
                 )
 
     gather_inner(0)
@@ -379,35 +361,41 @@
     def moment(index, one, two):
         total = zero
         for c in range(3):
-            for t in range(3):
-                rows = pl.ds(24 * c + 8 * t, 8)
+            for t in range(2):
+                rows = pl.ds(16 * c + 8 * t, 8)
                 total = total + weight_scr[pl.ds(8 * t, 8), :] * q_scr[one, rows, :] * q_scr[two, rows, :]
         moment_scr[pl.ds(index, 1), :] = jnp.sum(total, axis=0, keepdims=True)
 
     def write_basis(turn):
         for t in range(2):
             where_t = map_scr[pl.ds(8 * t, 8), :]
-            rows_t, lanes_t = (where_t >> 6) - 1, where_t & 63
+            rows_t, lanes_t = (where_t >> 7) - 1, where_t & 127
             for c in range(3):
-                inner = q_scr[turn, pl.ds(24 * c + 8 + 8 * t, 8), :]
-                value = pick(q_scr.at[turn], 24 * c, 8, 0, rows_t, lanes_t, inner)
-                for r in range(8 if t == 0 else 4):
-                    basis_scr[turn, pl.ds(c, 1), 128 * (8 * t + r) : 128 * (8 * t + r) + 128] = (
-                        value[r : r + 1, :]
-                    )
+                inner = q_scr[turn, pl.ds(16 * c + 8 * t, 8), :]
+                value = pick(q_scr.at[turn], 16 * c, BASE, 0, rows_t, lanes_t, inner)
+                for row in range(BASE if t == 0 else 0, 8):
+                    start = 128 * (8 * t + row - BASE)
+                    basis_scr[turn, pl.ds(c, 1), start : start + 128] = value[row : row + 1, :]
 
     def receive(turn, is_first):
         wait_halo(turn)
-        for c in range(3):
-            for j in range(PEERS):
-                in_scr[pl.ds(8 * c + j, 1), :] = recv_buf[turn, j, c]
-        for c in range(3):
-            value = own_scr[pl.ds(8 * c, 8), :] + in_scr[pl.ds(8 * c, 8), :]
+        lanes = lax.broadcasted_iota(jnp.int32, (1, 128), 1)
+        for c in range(3):
+            arrived = [recv_buf[turn, j, c] for j in range(PEERS)]
+            for row in range(BASE):
+                own = [j for j in range(PEERS) if PEER_ROW[j] == row]
+                own.sort(key=lambda j: PEER_LANE[j])
+                value = arrived[own[0]]
+                for j in own[1:]:
+                    value = jnp.where(lanes >= PEER_LANE[j], arrived[j], value)
+                in_scr[pl.ds(8 * c + row, 1), :] = value
+        for c in range(3):
+            value = own_scr[pl.ds(8 * c, BASE), :] + in_scr[pl.ds(8 * c, BASE), :]
             if not is_first:
-                before = q_scr[turn - 1, pl.ds(24 * c, 8), :]
-                scale = spread(scale_scr, 0)
+                before = q_scr[turn - 1, pl.ds(16 * c, BASE), :]
+                scale = jnp.broadcast_to(scale_scr[0:1, :], (BASE, 128))
                 value = value * scale + before * (DAMPING * scale - 1.0)
-            q_scr[turn, pl.ds(24 * c, 8), :] = value
+            q_scr[turn, pl.ds(16 * c, BASE), :] = value
 
     def stresses(turn):
         for t in range(4):
@@ -416,8 +404,8 @@
             for c in range(3):
                 u_scr[pl.ds(8 * t, 8), 128 * c : 128 * c + 128] = pick(
                     q_scr.at[turn],
-                    24 * c,
-                    8,
+                    16 * c,
+                    BASE,
                     0,
                     rows_t,
                     lanes_t,
@@ -449,51 +437,69 @@
         for p, part in enumerate(parts_of(summed)):
             t_scr[p] = part
 
-    def scatter(target, first, height):
-        numbers = lax.broadcasted_iota(jnp.int32, (height, 128), 0) + first
+    def term(p, a, c, height):
+        row = t_scr[p, pl.ds(a, 1), 128 * c : 128 * c + 128]
+        return jnp.broadcast_to(row, (height, 128))
+
+    def by_lane(left):
+        summed = None
+        for a in range(0, 27, 4):
+            part = jnp.dot(
+                jnp.concatenate(left[a : a + 4], axis=1),
+                hot_scr[128 * a : 128 * min(a + 4, 27), :],
+                preferred_element_type=F32,
+            )
+            summed = part if summed is None else summed + part
+        return summed
+
+    def scatter_shared(turn):
+        order = [(c, p) for c in range(3) for p in range(3)]
+        upper = sublane < BASE
+        numbers = sublane & (BASE - 1)
+        left = []
         for a in range(27):
-            mask = jnp.broadcast_to(row_scr[pl.ds(a, 1), :], (height, 128)) == numbers
-            groups = [
-                jnp.where(
-                    mask,
-                    jnp.broadcast_to(t_scr[p, pl.ds(a, 1), 128 * c : 128 * c + 128], (height, 128)),
-                    0.0,
-                )
-                for c in range(3)
-                for p in range(3)
-            ]
-            if height == 8:
-                groups.append(jnp.zeros((8, 128), F32))
-                groups = [
-                    jnp.concatenate(groups[i : i + 2], axis=0) for i in range(0, len(groups), 2)
-                ]
-            for i, group in enumerate(groups):
-                target[16 * i : 16 * i + 16, 128 * a : 128 * a + 128] = group.astype(BF16)
-        summed = jnp.dot(target[...], hot_scr[...], preferred_element_type=F32)
-        return [
-            summed[3 * height * c : 3 * height * c + height]
-            + summed[3 * height * c + height : 3 * height * c + 2 * height]
-            + summed[3 * height * c + 2 * height : 3 * height * c + 3 * height]
-            for c in range(3)
-        ]
-
-    def scatter_shared(turn):
-        for c, value in enumerate(scatter(rs_scr, 0, 8)):
-            own_scr[pl.ds(8 * c, 8), :] = value
+            mask = spread(row_scr, a) == numbers
+            tiles = []
+            for i in range(0, 9, 2):
+                value = term(order[i][1], a, order[i][0], 8)
+                if i < 8:
+                    other = term(order[i + 1][1], a, order[i + 1][0], 8)
+                    tiles.append(jnp.where(mask, jnp.where(upper, value, other), 0.0))
+                else:
+                    tiles.append(jnp.where(mask & upper, value, 0.0))
+            tiles.append(zero)
+            left.append(jnp.concatenate(tiles, axis=0).astype(BF16))
+        summed = by_lane(left)
+        for c in range(3):
+            own_scr[pl.ds(8 * c, BASE), :] = (
+                summed[12 * c : 12 * c + 4]
+                + summed[12 * c + 4 : 12 * c + 8]
+                + summed[12 * c + 8 : 12 * c + 12]
+            )
         fill_message(turn + 1)
         send_halo(turn + 1)
 
+    def scatter_inner():
+        left = []
+        for a in range(27):
+            mask = jnp.broadcast_to(row_scr[pl.ds(a, 1), :], (16, 128)) == sublane16
+            tiles = [jnp.where(mask, term(p, a, c, 16), 0.0) for c in range(3) for p in range(3)]
+            left.append(jnp.concatenate(tiles, axis=0).astype(BF16))
+        summed = by_lane(left)
+        for c in range(3):
+            inner_scr[pl.ds(16 * c, 16), :] = (
+                summed[48 * c : 48 * c + 16]
+                + summed[48 * c + 16 : 48 * c + 32]
+                + summed[48 * c + 32 : 48 * c + 48]
+            )
+
     def inner_rows(turn):
         scale = jnp.broadcast_to(scale_scr[0:1, :], (16, 128))
         for c in range(3):
-            rows = pl.ds(24 * c + 8, 16)
-            q_scr[turn + 1, rows, :] = inner_scr[pl.ds(16 * c, 16), :] * scale + q_scr[
-                turn, rows, :
-            ] * (DAMPING * scale - 1.0)
-
-    def scatter_inner():
-        for c, value in enumerate(scatter(ri_scr, 8, 16)):
-            inner_scr[pl.ds(16 * c, 16), :] = value
+            rows = pl.ds(16 * c, 16)
+            q_scr[turn + 1, rows, :] = inner_scr[rows, :] * scale + q_scr[turn, rows, :] * (
+                DAMPING * scale - 1.0
+            )
 
     def turn_of(turn, is_first):
         receive(turn, is_first)
@@ -590,7 +596,7 @@
         out_ref[1, :, 128 * r : 128 * r + width] = left[0:3, 0:width]
 
     for turn in range(ITERS + 1):
-        pltpu.make_async_copy(send_buf.at[turn], send_buf.at[turn], halo_send.at[turn]).wait()
+        pltpu.make_async_copy(recv_buf.at[turn], recv_buf.at[turn], halo_send.at[turn]).wait()
     for which in range(2):
         for stage in range(2):
             arrived = sum_in[stage].at[which]
@@ -599,7 +605,7 @@
 
 def shards(count, rhs_partial, connectivity, hessians, shared_nodes, owner):
     first, second = tables()
-    sizes = [int(np.prod([d for _, d in digits])) - 1 for digits in stage_digits(count)]
+    sizes = [len(masks) for masks in stage_masks(count)]
     vmem = pltpu.VMEM
     out = pl.pallas_call(
         functools.partial(kernel, count),
@@ -634,13 +640,11 @@
             vmem((96, 384), F32),
             vmem((288, 384), BF16),
             vmem((3, 32, 384), F32),
-            vmem((80, 27 * 128), BF16),
-            vmem((144, 27 * 128), BF16),
             vmem((ROWS, 128), F32),
             vmem((16, 128), F32),
             vmem((8, 128), F32),
             vmem((ITERS + 1, 8, NODE_ROWS * 128), F32),
-            vmem((ITERS + 1, PEERS, 3, 1, 128), F32),
+            vmem((ITERS + 1, BASE, 3, 1, 128), F32),
             vmem((ITERS + 1, PEERS, 3, 1, 128), F32),
             vmem((4, 1, 128), F32),
             vmem((2, sizes[0], 1, 128), F32),

time: 59.3 us -> 58.4 us (0.985)
  Pallas kernels: 57.9 us -> 57 us
    pallas_call x1, Pallas kernels: 57.9 us -> 57 us  [shards(): pl.pallas_call(functools.partial(kernel, count), out_shape=vmem((2, 3, NO...]
where the time goes in v3:
time: 58.4 us; the launch traced here: 58.3 us
  Pallas kernels  57 us (98%)
  between operations  0.64 us (1%)
  local copies, waits for them, and re-layouts  0.62 us (1%)
    pallas_call x1, Pallas kernels, shards(): pl.pallas_call(functools.partial(kernel, count), out_shape=vmem((2, 3, NO...  57 us

profile of v3, /device:TPU:1, one launch (start us, length us, event | category | flops | bytes accessed | tf_op | source)
XLA Modules:
  0.0 58.3 jit_solution(8441970847943387993)
XLA Ops:
  0.6 57.0 %newton_cg.1 = f32[2,3,1445]{2,1,0:T(4,128)S(1)} custom-call(f32[3,1445]{1,0:T(4,128)} %rhs_hbm.1, s32[27,128]{1,0:T(8,128)} %conn_hbm.1, bf16[27,45,128]{2,1,0:T(8,128)(2,1)} %bitcast.5, s32[8,34]{1,0:T(8,128)} %shared_hbm.1, s32[1445]{0:T(1024)} %owner_hbm.1, bf16[112,192]{1,0:T(8,128)(2,1)} %constant.4.clone.first_hbm, ...), custom_call_target="tpu_custom_call" | custom-call | tf_op jit(solution)/shard_map/newton_cg/pallas_call | solution.py:610
  57.7 0.6 %slice_bitcast_fusion = (f32[3,1445]{1,0:T(4,128)}, f32[3,1445]{1,0:T(4,128)}) fusion(f32[2,3,1445]{2,1,0:T(4,128)S(1)} %newton_cg.1), kind=kLoop, calls=%fused_computation | loop fusion | bytes 69360 | tf_op jit(solution)/shard_map/squeeze | solution.py:668

commit v4 on v3

--- a/solution.py
+++ b/solution.py
@@ -23,6 +23,7 @@
 SHARE = 34
 PEER_ROW = [0, 0, 0, 2, 3, 1, 1, 1]
 PEER_LANE = [0, 40, 80, 0, 0, 80, 40, 0]
+SEND_ORDER = [0, 7, 1, 6, 2, 5, 3, 4]
 SHIFT_SCALE = 0.045
 
 
@@ -93,10 +94,16 @@
     return [offset - half for offset in range(half)] + [offset + 1 for offset in range(half)]
 
 
+def links(mask):
+    ring = [0, 1, 2, 3, 4, 3, 2, 3]
+    return ring[(mask >> 1) & 7] + ring[(mask >> 4) & 7] + [0, 1, 2, 1][(mask >> 7) & 3]
+
+
 def stage_masks(count):
     bits = count.bit_length() - 1
     low = 1 << min(4, bits - 1)
-    return [list(range(1, low)), [low * k for k in range(1, count // low)]]
+    masks = [list(range(1, low)), [low * k for k in range(1, count // low)]]
+    return [sorted(stage, key=lambda mask: -links(mask)) for stage in masks]
 
 
 def parts_of(value):
@@ -205,7 +212,7 @@
     sublane16 = lax.broadcasted_iota(jnp.int32, (16, 128), 0)
 
     def send_halo(turn):
-        for j in range(PEERS):
+        for j in SEND_ORDER:
             pltpu.make_async_remote_copy(
                 src_ref=send_buf.at[turn, PEER_ROW[j]],
                 dst_ref=recv_buf.at[turn, PEERS - 1 - j],
@@ -533,9 +540,10 @@
     receive(last, False)
     moment(2 * last - 1, last - 1, last)
     moment(2 * last, last, last)
-    energy = stresses(last)
-    moment_scr[pl.ds(2 * last + 1, 1), :] = jnp.sum(energy, axis=0, keepdims=True)
-    send_sum(1, 0, row_of(moment_scr[...]))
+    known = row_of(moment_scr[...])
+    energy = jnp.sum(stresses(last), axis=0, keepdims=True)
+    total = jnp.sum(energy, axis=1, keepdims=True)
+    send_sum(1, 0, jnp.where(lane[0:1, :] == 2 * last + 1, total, known))
     terms()
     scatter_shared(last)
     scatter_inner()

time: 58.4 us -> 58.1 us (level)
  no operation moved by 1% of the time
where the time goes in v4:
time: 58.1 us; the launch traced here: 58 us
  Pallas kernels  56.8 us (98%)
  between operations  0.64 us (1%)
  local copies, waits for them, and re-layouts  0.62 us (1%)
    pallas_call x1, Pallas kernels, shards(): pl.pallas_call(functools.partial(kernel, count), out_shape=vmem((2, 3, NO...  56.8 us

profile of v4, /device:TPU:1, one launch (start us, length us, event | category | flops | bytes accessed | tf_op | source)
XLA Modules:
  0.0 58.0 jit_solution(10695229405503958982)
XLA Ops:
  0.6 56.8 %newton_cg.1 = f32[2,3,1445]{2,1,0:T(4,128)S(1)} custom-call(f32[3,1445]{1,0:T(4,128)} %rhs_hbm.1, s32[27,128]{1,0:T(8,128)} %conn_hbm.1, bf16[27,45,128]{2,1,0:T(8,128)(2,1)} %bitcast.5, s32[8,34]{1,0:T(8,128)} %shared_hbm.1, s32[1445]{0:T(1024)} %owner_hbm.1, bf16[112,192]{1,0:T(8,128)(2,1)} %constant.4.clone.first_hbm, ...), custom_call_target="tpu_custom_call" | custom-call | tf_op jit(solution)/shard_map/newton_cg/pallas_call | solution.py:618
  57.4 0.6 %slice_bitcast_fusion = (f32[3,1445]{1,0:T(4,128)}, f32[3,1445]{1,0:T(4,128)}) fusion(f32[2,3,1445]{2,1,0:T(4,128)S(1)} %newton_cg.1), kind=kLoop, calls=%fused_computation | loop fusion | bytes 69360 | tf_op jit(solution)/shard_map/squeeze | solution.py:676

commit v5 on v4

--- a/solution.py
+++ b/solution.py
@@ -283,7 +283,7 @@
         load.wait()
     for q in range(27):
         wide_scr[48 * q : 48 * q + 45, :] = hess_ref[q].astype(F32)
-    wide_scr[48 * 27 :, :] = jnp.zeros((48 * 5, 128), F32)
+    wide_scr[48 * 27 : 48 * 32, :] = jnp.zeros((48 * 5, 128), F32)
     for k in range(45):
         for t in range(4):
             h_scr[k, 8 * t : 8 * t + 8, :] = wide_scr[pl.ds(48 * 8 * t + k, 8, stride=48), :]
@@ -637,7 +637,7 @@
             vmem((32, 128), jnp.int32),
             vmem((32, 128), jnp.int32),
             vmem((27 * 128, 128), BF16),
-            vmem((48 * 32, 128), F32),
+            vmem((48 * 33, 128), F32),
             vmem((45, 32, 128), F32),
             vmem((ITERS + 1, 3 * ROWS, 128), F32),
             vmem((24, 128), F32),

time: 58.1 us -> 58.2 us (level)
  no operation moved by 1% of the time
where the time goes in v5:
time: 58.2 us; the launch traced here: 58 us
  Pallas kernels  56.8 us (98%)
  between operations  0.64 us (1%)
  local copies, waits for them, and re-layouts  0.62 us (1%)
    pallas_call x1, Pallas kernels, shards(): pl.pallas_call(functools.partial(kernel, count), out_shape=vmem((2, 3, NO...  56.8 us

profile of v5, /device:TPU:1, one launch (start us, length us, event | category | flops | bytes accessed | tf_op | source)
XLA Modules:
  0.0 58.0 jit_solution(16958162016738840049)
XLA Ops:
  0.6 56.8 %newton_cg.1 = f32[2,3,1445]{2,1,0:T(4,128)S(1)} custom-call(f32[3,1445]{1,0:T(4,128)} %rhs_hbm.1, s32[27,128]{1,0:T(8,128)} %conn_hbm.1, bf16[27,45,128]{2,1,0:T(8,128)(2,1)} %bitcast.5, s32[8,34]{1,0:T(8,128)} %shared_hbm.1, s32[1445]{0:T(1024)} %owner_hbm.1, bf16[112,192]{1,0:T(8,128)(2,1)} %constant.4.clone.first_hbm, ...), custom_call_target="tpu_custom_call" | custom-call | tf_op jit(solution)/shard_map/newton_cg/pallas_call | solution.py:618
  57.4 0.6 %slice_bitcast_fusion = (f32[3,1445]{1,0:T(4,128)}, f32[3,1445]{1,0:T(4,128)}) fusion(f32[2,3,1445]{2,1,0:T(4,128)S(1)} %newton_cg.1), kind=kLoop, calls=%fused_computation | loop fusion | bytes 69360 | tf_op jit(solution)/shard_map/squeeze | solution.py:676

commit v6 on v5

--- a/solution.py
+++ b/solution.py
@@ -463,8 +463,9 @@
         order = [(c, p) for c in range(3) for p in range(3)]
         upper = sublane < BASE
         numbers = sublane & (BASE - 1)
+        order_a = [a for a in range(27) if a not in (12, 13)] + [12]
         left = []
-        for a in range(27):
+        for a in order_a:
             mask = spread(row_scr, a) == numbers
             tiles = []
             for i in range(0, 9, 2):
@@ -476,7 +477,15 @@
                     tiles.append(jnp.where(mask & upper, value, 0.0))
             tiles.append(zero)
             left.append(jnp.concatenate(tiles, axis=0).astype(BF16))
-        summed = by_lane(left)
+        summed = None
+        for i in range(0, 26, 2):
+            table = [hot_scr[128 * a : 128 * a + 128, :] for a in order_a[i : i + 2]]
+            part = jnp.dot(
+                jnp.concatenate(left[i : i + 2], axis=1),
+                jnp.concatenate(table, axis=0),
+                preferred_element_type=F32,
+            )
+            summed = part if summed is None else summed + part
         for c in range(3):
             own_scr[pl.ds(8 * c, BASE), :] = (
                 summed[12 * c : 12 * c + 4]

time: 58.2 us -> 58.1 us (level)
  no operation moved by 1% of the time
where the time goes in v6:
time: 58.1 us; the launch traced here: 58 us
  Pallas kernels  56.7 us (98%)
  between operations  0.64 us (1%)
  local copies, waits for them, and re-layouts  0.62 us (1%)
    pallas_call x1, Pallas kernels, shards(): pl.pallas_call(functools.partial(kernel, count), out_shape=vmem((2, 3, NO...  56.7 us

profile of v6, /device:TPU:1, one launch (start us, length us, event | category | flops | bytes accessed | tf_op | source)
XLA Modules:
  0.0 58.0 jit_solution(1945509537762331753)
XLA Ops:
  0.6 56.7 %newton_cg.1 = f32[2,3,1445]{2,1,0:T(4,128)S(1)} custom-call(f32[3,1445]{1,0:T(4,128)} %rhs_hbm.1, s32[27,128]{1,0:T(8,128)} %conn_hbm.1, bf16[27,45,128]{2,1,0:T(8,128)(2,1)} %bitcast.5, s32[8,34]{1,0:T(8,128)} %shared_hbm.1, s32[1445]{0:T(1024)} %owner_hbm.1, bf16[112,192]{1,0:T(8,128)(2,1)} %constant.4.clone.first_hbm, ...), custom_call_target="tpu_custom_call" | custom-call | tf_op jit(solution)/shard_map/newton_cg/pallas_call | solution.py:627
  57.4 0.6 %slice_bitcast_fusion = (f32[3,1445]{1,0:T(4,128)}, f32[3,1445]{1,0:T(4,128)}) fusion(f32[2,3,1445]{2,1,0:T(4,128)S(1)} %newton_cg.1), kind=kLoop, calls=%fused_computation | loop fusion | bytes 69360 | tf_op jit(solution)/shard_map/squeeze | solution.py:685
